TPU v7x, 512 devices: a whole 4x8x8 slice. The times are simulated.
512 devices in a mesh: cfg: 64 (over y, x, core), tp: 8 (over z).
Axes of the slice: x: 4, y: 8, z: 8, core: 2. Of those that a mesh axis runs over, the one named last changes fastest.
Arguments:
- pool: bfloat16 [64, 192, 8192], P('cfg', None, 'tp'), may hold values from -6 to 6
- base_run: int32 [1], replicated, may hold values from 0 to 63
- gain: bfloat16 [8192], replicated, may hold values from 0.099609375 to 1.8984375
- w_key: bfloat16 [8192, 1024], P(None, 'tp'), may hold values from -0.0625 to 0.0625
- w_value: bfloat16 [8192, 1024], P(None, 'tp'), may hold values from -0.0625 to 0.0625
- w_query: bfloat16 [8192, 8192], P('cfg', 'tp'), may hold values from -0.0625 to 0.0625
- src_pos: int32 [192, 64, 2], P(None, 'cfg'), may hold values from 0 to 191
- dst_pos: int32 [192, 64, 2], P('cfg'), may hold values from 0 to 187, as said below
- counts: int32 [192, 64], P('cfg'), may hold values from 0 to 2
Outputs:
- attended: bfloat16 [192, 4, 8192], P('cfg', None, 'tp')
- keys: bfloat16 [192, 192, 1024], P('cfg', None, 'tp')
- values: bfloat16 [192, 192, 1024], P('cfg', None, 'tp')
Inputs may be any that keep to these rules, and one draw needn't show every extreme that they name: `dst_pos`: within one config all 128 entries differ and lie below 188. `counts`: slots of config c and source run s in use, the first ones of the 2.
All inputs are finite; a program needn't handle non-finite values.
Results may differ from a plain program's by a relative error of at most 0.023.
Values may be sent and summed in bfloat16 or wider, within the bound.
A program may use at most 64 MiB of HBM per device.

v0:
```python
import math

import jax
import jax.numpy as jnp
from jax import lax
from jax.sharding import PartitionSpec as P

D = 8192
HD = 128
PROBE = 4


rope_base = 500000.0
epsilon = 1e-05


def spread(value, axis, source):
    kept = jnp.where(lax.axis_index(axis) == source, value, 0).astype(value.dtype)
    return lax.psum(kept, axis)


def rotate(tensor, positions):
    half_dim = tensor.shape[-1] // 2
    inverse_freq = jnp.exp(
        jnp.arange(half_dim, dtype=jnp.float32) * (-2.0 * math.log(rope_base) / tensor.shape[-1])
    )
    angles = positions.astype(jnp.float32)[:, None] * inverse_freq[None, :]
    cosine = jnp.cos(angles)[:, None, :]
    sine_vals = jnp.sin(angles)[:, None, :]
    lower_half = tensor[..., :half_dim]
    upper_half = tensor[..., half_dim:]
    return jnp.concatenate(
        [
            lower_half * cosine - upper_half * sine_vals,
            upper_half * cosine + lower_half * sine_vals,
        ],
        axis=-1,
    )


def body(pool, base_run, gain, w_key, w_value, w_query, src_pos, dst_pos, counts):
    length = pool.shape[1]
    local_cfg = dst_pos.shape[0]
    slot_count = dst_pos.shape[1] * dst_pos.shape[2]
    key_cols = w_key.shape[1]
    in_use = jnp.arange(dst_pos.shape[2], dtype=jnp.int32)[None, None, :] < counts[:, :, None]
    targets = jnp.where(in_use, dst_pos, length).reshape(local_cfg, slot_count)
    onehot = targets[:, :, None] == jnp.arange(length, dtype=jnp.int32)[None, None, :]
    covered = jnp.any(onehot, axis=1)
    base_rows = spread(pool[0], "cfg", base_run[0])
    picked = jnp.take(pool[0], src_pos[:, 0, :], axis=0)[:, None]
    arrived = lax.all_to_all(picked, "cfg", split_axis=0, concat_axis=1, tiled=True)
    arrived = arrived.reshape(local_cfg, slot_count, arrived.shape[-1])
    spliced = jnp.einsum(
        "csp,csd->cpd", onehot.astype(jnp.bfloat16), arrived, preferred_element_type=jnp.float32
    )
    patched = jnp.where(covered[:, :, None], spliced, base_rows[None].astype(jnp.float32)).astype(
        jnp.bfloat16
    )
    rows = patched.reshape(local_cfg * length, patched.shape[-1])
    gains = gain.astype(jnp.float32)
    widened = lax.all_gather(rows, "tp", axis=1, tiled=True).astype(jnp.float32)
    normed = (widened * gains[None, :]).astype(jnp.bfloat16)
    keys_acc = jnp.dot(normed, w_key, preferred_element_type=jnp.float32)
    values_acc = jnp.dot(normed, w_value, preferred_element_type=jnp.float32)
    squares = jnp.sum(widened * widened, axis=1)
    probe_rows = normed[length - PROBE : length]
    keys_acc, values_acc, squares, probe_rows = (keys_acc, values_acc, squares, probe_rows)
    scales = lax.rsqrt(squares / D + epsilon)
    key_raw = (scales[:, None] * keys_acc).reshape(local_cfg, length, key_cols)
    value_raw = (scales[:, None] * values_acc).reshape(local_cfg, length, key_cols)
    probe_scales = scales[length - PROBE : length]
    slice_rows = w_query.shape[0]
    probe_part = lax.dynamic_slice_in_dim(
        probe_rows, lax.axis_index("cfg") * slice_rows, slice_rows, 1
    )
    partial_value = jnp.dot(probe_part, w_query, preferred_element_type=jnp.float32)
    query_total = lax.psum(partial_value, "cfg")
    heads_dev = w_query.shape[1] // HD
    kv_dev = key_cols // HD
    group_size = heads_dev // kv_dev
    positions = jnp.arange(length, dtype=jnp.int32)
    probe_pos = length - PROBE + jnp.arange(PROBE, dtype=jnp.int32)
    queries = rotate(
        (probe_scales[:, None] * query_total).reshape(PROBE, heads_dev, HD), probe_pos
    ).astype(jnp.bfloat16)
    keys_out = rotate(key_raw.reshape(local_cfg, length, kv_dev, HD), positions).astype(
        jnp.bfloat16
    )
    values_out = value_raw.astype(jnp.bfloat16)
    query_groups = queries.reshape(PROBE, kv_dev, group_size, HD)
    value_heads = values_out.reshape(local_cfg, length, kv_dev, HD)
    scores = jnp.einsum(
        "pkgh,cskh->cpkgs", query_groups, keys_out, preferred_element_type=jnp.float32
    ) * HD ** (-0.5)
    causal = positions[None, :] <= probe_pos[:, None]
    scores = jnp.where(causal[None, :, None, None, :], scores, -1e30)
    probs_b = jax.nn.softmax(scores, axis=-1).astype(jnp.bfloat16)
    attended = jnp.einsum(
        "cpkgs,cskh->cpkgh", probs_b, value_heads, preferred_element_type=jnp.float32
    )
    attended = attended.astype(jnp.bfloat16).reshape(local_cfg, PROBE, heads_dev * HD)
    return (attended, keys_out.reshape(local_cfg, length, key_cols), values_out)


def solution(mesh):
    placed = (
        P("cfg", None, "tp"),
        P(),
        P(),
        P(None, "tp"),
        P(None, "tp"),
        P("cfg", "tp"),
        P(None, "cfg", None),
        P("cfg", None, None),
        P("cfg", None),
    )
    return jax.shard_map(
        body,
        mesh=mesh,
        in_specs=placed,
        out_specs=(P("cfg", None, "tp"), P("cfg", None, "tp"), P("cfg", None, "tp")),
        check_vma=False,
    )
```

profile of v0, /device:TPU:1, one launch (start us, length us, event | category | flops | bytes accessed | tf_op | source)
XLA Modules:
  0.0 616.7 jit_solution(13707132915547980617)
XLA Ops:
  7.2 0.8 compare_select_fusion
  8.0 0.7 compare_and_fusion
  9.0 3.8 gather_fusion
  12.9 1.2 gather.7
  14.2 2.7 broadcast_select_fusion
  16.9 11.6 %all-to-all-start = ((bf16[192,1,2,1024]{3,2,1,0:T(2,128)(2,1)}), bf16[192,1,2,1024]{3,2,1,0:T(2,128)(2,1)S(1)}, u32[]{:S(2)}, u32[]{:S(2)}) async-start(bf16[192,1,2,1024]{3,2,1,0:T(2,128)(2,1)} %broadcast_select_fusion), calls=%async_computation | async-start | bytes 1572864 | tf_op jit(solution)/shard_map/all_to_all | solution.py:52
  29.2 0.8 broadcast_select_fusion.1
  30.4 0.2 fusion.6
  30.6 20.7 %all-to-all-done = bf16[192,1,2,1024]{3,2,1,0:T(2,128)(2,1)S(1)} async-done(((bf16[192,1,2,1024]{3,2,1,0:T(2,128)(2,1)}), bf16[192,1,2,1024]{3,2,1,0:T(2,128)(2,1)S(1)}, u32[]{:S(2)}, u32[]{:S(2)}) %all-to-all-start) | async-done | bytes 786464 | tf_op jit(solution)/shard_map/all_to_all | solution.py:52
  51.3 1.4 copy.21
  52.7 2.3 reshape.261
  54.9 172.0 %all-reduce.2.cloned.1.call-done = bf16[192,1024]{1,0:T(8,128)(2,1)} async-done(((bf16[192,1024]{1,0:T(8,128)(2,1)}), bf16[192,1024]{1,0:T(8,128)(2,1)}) %all-reduce.2.cloned.1.call-update) | async-done | bytes 393232 | tf_op jit(solution)/shard_map/psum | solution.py:19
  227.0 2.5 select_convert_fusion
  229.7 0.4 multiply_cosine_fusion
  230.2 107.6 %all-gather.2.cloned.1.call-done = bf16[576,8192]{1,0:T(8,128)(2,1)} async-done(((bf16[576,1024]{1,0:T(8,128)(2,1)}), bf16[576,8192]{1,0:T(8,128)(2,1)}) %all-gather.2.cloned.1.call-update) | async-done | bytes 9437200 | tf_op jit(solution)/shard_map/all_gather | solution.py:62
  337.8 11.2 %fusion = (f32[576]{0:T(1024)S(1)}, bf16[576,8192]{1,0:T(8,128)(2,1)}) fusion(bf16[576,8192]{1,0:T(8,128)(2,1)} %all-gather.2.cloned.1.call-done, f32[8192]{0:T(1024)S(1)} %convert_element_type.76), kind=kLoop, calls=%fused_computation.3 | loop fusion | flops 23592384 | bytes 18909440 | tf_op jit(solution)/shard_map/reduce_sum | solution.py:66
  349.0 1.0 slice.28
  350.1 5.2 convolution_multiply_fusion
  355.4 245.7 %psum.15 = f32[4,1024]{1,0:T(4,128)S(1)} all-reduce(f32[4,1024]{1,0:T(4,128)S(1)} %fusion.16), channel_id=1, replica_groups=mesh['cfg'=64,'tp'=8] {'cfg'}, use_global_device_ids=true, to_apply=%region_3.4 | all-reduce | flops 4096 | bytes 32768 | tf_op jit(solution)/shard_map/psum | solution.py:78
  601.2 6.9 %fusion.2 = bf16[576,128]{1,0:T(8,128)(2,1)S(1)} fusion(bf16[576,8192]{1,0:T(8,128)(2,1)} %get-tuple-element.4, bf16[8192,128]{1,0:T(8,128)(2,1)} %param.13, f32[576]{0:T(1024)S(1)} %add_rsqrt_fusion), kind=kOutput, calls=%fused_computation.9 | convolution fusion | flops 1208107008 | bytes 11684096 | tf_op jit(solution)/shard_map/dot_general | solution.py:65
  608.5 0.3 fusion.21
  608.8 0.2 fusion.11
  609.0 0.2 fusion.5
  609.2 0.6 reshape.265
  (42 shorter events, 1.7 us)
Async XLA Ops:
  7.2 342.9 %copy-start = (bf16[8192,128]{1,0:T(8,128)(2,1)S(1)}, bf16[8192,128]{1,0:T(8,128)(2,1)}, u32[]{:S(2)}) copy-start(bf16[8192,128]{1,0:T(8,128)(2,1)} %param.12) | copy-start | bytes 6291460
  7.2 22.0 %copy-start.1 = (bf16[1,192,1024]{2,1,0:T(8,128)(2,1)S(1)}, bf16[1,192,1024]{2,1,0:T(8,128)(2,1)}, u32[]{:S(2)}) copy-start(bf16[1,192,1024]{2,1,0:T(8,128)(2,1)} %param.9) | copy-start | bytes 1179652
  7.2 22.9 %copy-start.5 = (s32[3,64,2]{1,2,0:T(2,128)S(1)}, s32[3,64,2]{1,2,0:T(2,128)}, u32[]{:S(2)}) copy-start(s32[3,64,2]{1,2,0:T(2,128)} %param.16) | copy-start | bytes 4612
  7.2 22.9 %copy-start.6 = (s32[3,64]{1,0:T(4,128)S(1)}, s32[3,64]{1,0:T(4,128)}, u32[]{:S(2)}) copy-start(s32[3,64]{1,0:T(4,128)} %param.17) | copy-start | bytes 2308
  9.0 220.5 %copy-start.4 = (bf16[8192]{0:T(1024)(128)(2,1)S(1)}, bf16[8192]{0:T(1024)(128)(2,1)}, u32[]{:S(2)}) copy-start(bf16[8192]{0:T(1024)(128)(2,1)} %param.11) | copy-start | bytes 49156
  16.9 34.4 %all-to-all-start = ((bf16[192,1,2,1024]{3,2,1,0:T(2,128)(2,1)}), bf16[192,1,2,1024]{3,2,1,0:T(2,128)(2,1)S(1)}, u32[]{:S(2)}, u32[]{:S(2)}) async-start(bf16[192,1,2,1024]{3,2,1,0:T(2,128)(2,1)} %broadcast_select_fusion), calls=%async_computation | async-start | bytes 1572864 | tf_op jit(solution)/shard_map/all_to_all | solution.py:52
  28.5 198.5 %all-reduce.2.cloned.1.call-start = ((), (), s32[]{:S(2)}) async-start(), calls=%async_computation.1 | async-start | bytes 786432 | tf_op jit(solution)/shard_map/psum | solution.py:19
  30.0 307.8 %all-gather.2.cloned.1.call-start = ((), (), s32[]{:S(2)}) async-start(), calls=%async_computation.2 | async-start | bytes 10616832 | tf_op jit(solution)/shard_map/all_gather | solution.py:62
  349.0 6.3 %copy-start.3 = (bf16[128,1024]{1,0:T(8,128)(2,1)S(1)}, bf16[128,1024]{1,0:T(8,128)(2,1)}, u32[]{:S(2)}) copy-start(bf16[128,1024]{1,0:T(8,128)(2,1)} %param.14) | copy-start | bytes 786436
  608.1 1.8 copy-start.7
  608.4 1.5 copy-start.2
Sparse Core Ops, SparseCore 0:
  32.8 194.1 all-reduce.1
  229.6 108.1 all-gather.1
where the time goes:
time: 619 us; the launch traced here: 617 us
  waiting for transfers between devices  300 us (48%)
  blocking collectives  246 us (40%)
  other arithmetic  17.6 us (3%)
  matrix products  15.3 us (2%)
  between operations  14.9 us (2%)
  starting transfers between devices  11.7 us (2%)
  local copies, waits for them, and re-layouts  11.1 us (2%)
    psum x1, blocking collectives, body(): query_total = lax.psum(partial_value, 'cfg')  246 us
    psum x1, waiting for transfers between devices, spread(): return lax.psum(kept, axis)  172 us
    all_gather x1, waiting for transfers between devices, body(): widened = lax.all_gather(rows, 'tp', axis=1, tiled=True).astype(jnp.float32)  108 us
    all_to_all x1, waiting for transfers between devices, body(): lax.all_to_all(picked, 'cfg', split_axis=0, concat_axis=1, tiled=True)  20.7 us
  transfers between devices with their start and end apart: 3, of which 3 were waited for; matrix products, arithmetic and copies ran while one was open for 1% of the time, Pallas kernels for 0%

commit v1 on v0

v1 whole, which is shorter than its diff:
```python
import functools
import math

import jax
import jax.numpy as jnp
import numpy as np
from jax import lax
from jax.experimental import pallas as pl
from jax.experimental.pallas import tpu as pltpu
from jax.sharding import PartitionSpec as P

HD = 128
PROBE = 4
TILE = 16
ROPE_BASE = 500000.0
EPSILON = 1e-05
MESH = pl.DeviceIdType.MESH
f32 = jnp.float32
bf16 = jnp.bfloat16


def rope_tables(first, count):
    half = HD // 2
    freq = np.exp(np.arange(half, dtype=np.float64) * (-2.0 * math.log(ROPE_BASE) / HD))
    angles = np.arange(first, first + count, dtype=np.float64)[:, None] * freq[None, :]
    cosine, sine = np.cos(angles), np.sin(angles)
    return np.stack(
        [np.concatenate([cosine, cosine], 1), np.concatenate([-sine, sine], 1)]
    ).astype(np.float32)


def rotate(rows, cosine, sine):
    return rows * cosine + pltpu.roll(rows, HD // 2, 1) * sine


def lane_groups(squares):
    total = squares[:, :HD]
    for k in range(1, squares.shape[1] // HD):
        total = total + squares[:, k * HD : (k + 1) * HD]
    return total


def gather_kernel(
    n_cfg,
    n_tp,
    pool,
    base,
    gain,
    w_key,
    w_value,
    w_query,
    picks,
    rope,
    arrived,
    base_kv,
    queries,
    rows,
    weights,
    wq,
    masked,
    landed,
    base_rows,
    block,
    part,
    parts,
    chosen,
    kv,
    outgoing,
    acc,
    sums,
    load_sem,
    ring_send,
    ring_recv,
    send,
    recv,
):
    cfg, tp = lax.axis_index("cfg"), lax.axis_index("tp")
    seq, width = rows.shape[1], rows.shape[2]
    half_rows = seq // 2
    model = n_tp * width
    heads = queries.shape[0]
    holders = seq // TILE
    spacing = n_cfg // holders
    is_holder = jnp.logical_and(lax.rem(cfg, spacing) == 0, cfg < holders * spacing)
    my_tile = cfg // spacing
    last_holder = (holders - 1) * spacing
    owner_step = (n_cfg - 1) // (heads - 1)
    is_owner = jnp.logical_and(lax.rem(cfg, owner_step) == 0, cfg < heads * owner_step)
    my_head = cfg // owner_step
    per_plane = n_cfg // n_tp

    loads = [
        pltpu.make_async_copy(pool, rows.at[tp], load_sem.at[0]),
        pltpu.make_async_copy(w_key, weights.at[:, pl.ds(0, HD)], load_sem.at[1]),
        pltpu.make_async_copy(w_value, weights.at[:, pl.ds(HD, HD)], load_sem.at[2]),
        pltpu.make_async_copy(w_query, wq, load_sem.at[3]),
    ]
    for load in loads:
        load.start()

    barrier = pltpu.get_barrier_semaphore()

    @pl.loop(1, n_cfg)
    def _(i):
        pl.semaphore_signal(
            barrier, inc=1, device_id={"cfg": lax.rem(cfg + i, n_cfg)}, device_id_type=MESH
        )

    @pl.loop(1, n_tp)
    def _(i):
        pl.semaphore_signal(
            barrier, inc=1, device_id={"tp": lax.rem(tp + i, n_tp)}, device_id_type=MESH
        )

    loads[0].wait()
    is_base = jnp.full((TILE, width), base[0], jnp.int32) == cfg
    for j in range(holders):
        mine = rows[tp, pl.ds(j * TILE, TILE), :].astype(f32)
        masked[j] = jnp.where(is_base, mine, 0.0).astype(bf16)
    pl.semaphore_wait(barrier, n_cfg - 1 + n_tp - 1)

    def to_cfg(src, dst, which, target):
        return pltpu.make_async_remote_copy(
            src_ref=src,
            dst_ref=dst,
            send_sem=send.at[which],
            recv_sem=recv.at[which],
            device_id={"cfg": target},
            device_id_type=MESH,
        )

    def settle(ref, sem):
        pltpu.make_async_copy(ref, ref, sem).wait()

    def ring(direction, unit):
        hop = unit // 2
        part_no = unit % 2 if direction == 0 else 1 - unit % 2
        sign = 1 if direction == 0 else -1
        slot = lax.rem(tp - sign * hop + n_tp, n_tp)
        piece = rows.at[slot, pl.ds(part_no * half_rows, half_rows)]
        return pltpu.make_async_remote_copy(
            src_ref=piece,
            dst_ref=piece,
            send_sem=ring_send.at[direction, unit],
            recv_sem=ring_recv.at[direction, unit],
            device_id={"tp": lax.rem(tp + sign + n_tp, n_tp)},
            device_id_type=MESH,
        )

    def gains(slot):
        return jnp.concatenate([gain[slot * per_plane + k] for k in range(per_plane)], axis=1)

    def project(slot, part_no):
        piece = pl.ds(part_no * half_rows, half_rows)
        wide = rows[slot, piece, :].astype(f32)
        sums[piece, :] += lane_groups(wide * wide)
        normed = (wide * gains(slot)).astype(bf16)
        depth = pl.ds(pl.multiple_of(slot * width, width), width)
        acc[piece, :] += jnp.dot(normed, weights[depth, :], preferred_element_type=f32)

    units = n_tp - 1

    def ring_step(unit):
        for direction in (0, 1):
            sign = 1 if direction == 0 else -1
            hop = unit // 2 + 1
            part_no = unit % 2 if direction == 0 else 1 - unit % 2
            slot = lax.rem(tp - sign * hop + n_tp, n_tp)
            piece = rows.at[slot, pl.ds(part_no * half_rows, half_rows)]
            pltpu.make_async_copy(piece, piece, ring_recv.at[direction, unit]).wait()
            if unit + 2 < units:
                ring(direction, unit + 2).start()
        for direction in (0, 1):
            sign = 1 if direction == 0 else -1
            hop = unit // 2 + 1
            part_no = unit % 2 if direction == 0 else 1 - unit % 2
            project(lax.rem(tp - sign * hop + n_tp, n_tp), part_no)

    for unit in range(min(2, units)):
        ring(0, unit).start()
        ring(1, unit).start()

    for j in range(holders):

        @pl.when(cfg != j * spacing)
        def _():
            to_cfg(masked.at[j], landed.at[cfg], 0, j * spacing).start()

    @pl.when(is_holder)
    def _():
        landed[cfg] = masked[my_tile]

    acc[...] = jnp.zeros_like(acc)
    sums[...] = jnp.zeros_like(sums)
    for load in loads[1:]:
        load.wait()
    project(tp, 0)
    project(tp, 1)
    column = lax.broadcasted_iota(jnp.int32, (TILE * 4, 2 * seq), 1)

    @pl.loop(0, n_cfg // 4)
    def _(i):
        span = pl.ds(pl.multiple_of(i * TILE * 4, TILE * 4), TILE * 4)
        chosen[span, :] = (column == picks[span, :]).astype(f32).astype(bf16)

    def base_arrives():
        @pl.when(is_holder)
        def _():
            settle(landed.at[pl.ds(0, n_cfg - 1)], recv.at[0])

            def add(s, total):
                return total + landed[s].astype(f32)

            total = lax.fori_loop(0, n_cfg, add, jnp.zeros((TILE, width), f32))
            base_rows[tp] = total.astype(bf16)

            @pl.loop(1, n_tp)
            def _(i):
                pltpu.make_async_remote_copy(
                    src_ref=base_rows.at[tp],
                    dst_ref=base_rows.at[tp],
                    send_sem=send.at[1],
                    recv_sem=recv.at[1],
                    device_id={"tp": lax.rem(tp + i, n_tp)},
                    device_id_type=MESH,
                ).start()

    def base_projects():
        @pl.when(is_holder)
        def _():
            settle(base_rows.at[pl.ds(0, n_tp - 1)], recv.at[1])

            @pl.when(cfg == last_holder)
            def _():
                @pl.loop(1, n_cfg)
                def _(i):
                    target = lax.rem(cfg + i, n_cfg)
                    lanes = pl.ds(pl.multiple_of(lax.rem(target, per_plane) * HD, HD), HD)
                    to_cfg(base_rows.at[target // per_plane, :, lanes], block, 2, target).start()

                lanes = pl.ds(pl.multiple_of(lax.rem(cfg, per_plane) * HD, HD), HD)
                block[...] = base_rows[cfg // per_plane, :, lanes]

            def add(z, state):
                total, squares = state
                wide = base_rows[z].astype(f32)
                normed = (wide * gains(z)).astype(bf16)
                depth = pl.ds(pl.multiple_of(z * width, width), width)
                total += jnp.dot(normed, weights[depth, :], preferred_element_type=f32)
                return total, squares + lane_groups(wide * wide)

            total, squares = lax.fori_loop(
                0, n_tp, add, (jnp.zeros((TILE, 2 * HD), f32), jnp.zeros((TILE, HD), f32))
            )
            scale = lax.rsqrt(jnp.sum(squares, axis=1, keepdims=True) / model + EPSILON)
            base_kv[my_tile] = (total * scale).astype(bf16)

            @pl.loop(1, n_cfg)
            def _(i):
                to_cfg(
                    base_kv.at[my_tile], base_kv.at[my_tile], 3, lax.rem(cfg + i, n_cfg)
                ).start()

    def query_parts():
        @pl.when(cfg != last_holder)
        def _():
            settle(block, recv.at[2])

        wide = block[...].astype(f32)
        normed = (wide * gain[cfg]).astype(bf16)
        total = jnp.dot(normed, wq[...], preferred_element_type=f32)
        squares = wide * wide
        for h in range(heads):
            part[h, pl.ds(0, 8), :] = total[8:, h * HD : (h + 1) * HD]
            part[h, pl.ds(8, 8), :] = squares[8:, :]
        for h in range(heads):

            @pl.when(cfg != h * owner_step)
            def _():
                to_cfg(part.at[h], parts.at[cfg], 4, h * owner_step).start()

        @pl.when(is_owner)
        def _():
            parts[cfg] = part[my_head]

    def query_sums():
        @pl.when(is_owner)
        def _():
            settle(parts.at[pl.ds(0, n_cfg - 1)], recv.at[4])

            def add(s, total):
                return total + parts[s]

            total = lax.fori_loop(0, n_cfg, add, jnp.zeros((TILE, HD), f32))
            scale = lax.rsqrt(jnp.sum(total[8:], axis=1, keepdims=True) / model + EPSILON)
            queries[my_head] = rotate(total[:8] * scale, rope[0], rope[1])

            @pl.loop(1, n_cfg)
            def _(i):
                to_cfg(
                    queries.at[my_head], queries.at[my_head], 5, lax.rem(cfg + i, n_cfg)
                ).start()

    beside = {1: base_arrives, 2: base_projects, 3: query_parts, 4: query_sums}
    for unit in range(units):
        ring_step(unit)
        if unit in beside:
            beside.pop(unit)()
    for unit in sorted(beside):
        beside[unit]()

    scale = lax.rsqrt(jnp.sum(sums[...], axis=1, keepdims=True) / model + EPSILON)
    scaled = (acc[...] * scale).astype(bf16)
    kv[pl.ds(0, seq), :] = scaled[:, :HD]
    kv[pl.ds(seq, seq), :] = scaled[:, HD:]
    picked = jnp.dot(chosen[...], kv[...], preferred_element_type=f32).astype(bf16)
    outgoing[...] = picked.reshape(n_cfg, TILE, HD)

    @pl.loop(1, n_cfg)
    def _(i):
        target = lax.rem(cfg + i, n_cfg)
        to_cfg(outgoing.at[target], arrived.at[cfg], 6, target).start()

    arrived[cfg] = outgoing[cfg]

    for unit in range(units):
        for direction in (0, 1):
            ring(direction, unit).wait_send()

    def both(condition, if_true, if_false):
        pl.when(condition)(if_true)
        pl.when(jnp.logical_not(condition))(if_false)

    both(
        is_holder,
        lambda: settle(masked.at[pl.ds(0, holders - 1)], send.at[0]),
        lambda: settle(masked, send.at[0]),
    )

    @pl.when(is_holder)
    def _():
        settle(base_rows.at[pl.ds(0, n_tp - 1)], send.at[1])
        settle(landed.at[pl.ds(0, n_cfg - 1), :, pl.ds(0, 2 * HD)], send.at[3])

    @pl.when(cfg == last_holder)
    def _():
        settle(arrived.at[pl.ds(0, n_cfg - 1)], send.at[2])

    both(
        is_owner,
        lambda: settle(part.at[pl.ds(0, heads - 1)], send.at[4]),
        lambda: settle(part, send.at[4]),
    )
    both(
        is_holder,
        lambda: settle(base_kv.at[pl.ds(0, holders - 1)], recv.at[3]),
        lambda: settle(base_kv, recv.at[3]),
    )
    both(
        is_owner,
        lambda: settle(queries.at[pl.ds(0, heads - 1)], recv.at[5]),
        lambda: settle(queries, recv.at[5]),
    )

    @pl.when(is_owner)
    def _():
        settle(arrived.at[pl.ds(0, n_cfg - 1)], send.at[5])

    settle(outgoing.at[pl.ds(0, n_cfg - 1)], send.at[6])
    settle(arrived.at[pl.ds(0, n_cfg - 1)], recv.at[6])


def attend_kernel(arrived, base_kv, queries, targets, rope, attended, keys, values):
    n_configs, seq = keys.shape[0], keys.shape[1]
    heads = queries.shape[0]
    spliced = arrived[...].astype(f32)
    slots = spliced.shape[0] * 8
    rows = jnp.concatenate(
        [spliced[:, :8, :].reshape(slots, HD), spliced[:, 8:, :].reshape(slots, HD)], axis=1
    ).astype(bf16)
    base = base_kv[...].reshape(seq, 2 * HD).astype(f32)
    probes = queries[...].reshape(heads * 8, HD).astype(bf16)
    position = lax.broadcasted_iota(jnp.int32, (seq, slots), 0)
    probe_row = lax.broadcasted_iota(jnp.int32, (heads * 8, seq), 0)
    causal = lax.broadcasted_iota(jnp.int32, (heads * 8, seq), 1) <= seq - 8 + lax.rem(probe_row, 8)
    cosine, sine = rope[0], rope[1]
    for i in range(n_configs):
        onehot = (position == targets[pl.ds(i, 1), :]).astype(f32)
        covered = jnp.max(onehot, axis=1, keepdims=True)
        taken = jnp.dot(onehot.astype(bf16), rows, preferred_element_type=f32)
        both = jnp.where(covered > 0.0, taken, base)
        key = rotate(both[:, :HD], cosine, sine).astype(bf16)
        value = both[:, HD:].astype(bf16)
        keys[i] = key
        values[i] = value
        scores = lax.dot_general(
            probes, key, (((1,), (1,)), ((), ())), preferred_element_type=f32
        ) * HD ** (-0.5)
        scores = jnp.where(causal, scores, -1e30)
        top = jnp.max(scores, axis=1, keepdims=True)
        grown = jnp.exp(scores - top)
        probs = (grown / jnp.sum(grown, axis=1, keepdims=True)).astype(bf16)
        out = jnp.dot(probs, value, preferred_element_type=f32)
        for h in range(heads):
            attended[i, :, h * HD : (h + 1) * HD] = out[h * 8 + 8 - PROBE : h * 8 + 8, :].astype(bf16)


def body(n_cfg, n_tp, pool, base_run, gain, w_key, w_value, w_query, src_pos, dst_pos, counts):
    seq, width = pool.shape[1], pool.shape[2]
    n_configs, cap = dst_pos.shape[0], dst_pos.shape[2]
    used = n_configs * cap
    heads = w_query.shape[1] // HD
    holders = seq // TILE
    gains = gain.astype(f32).reshape(n_cfg, 1, HD)
    wanted = src_pos.reshape(n_cfg, used)
    wanted = jnp.pad(wanted, ((0, 0), (0, 8 - used)), constant_values=-2 * seq)
    picks = jnp.concatenate([wanted, wanted + seq], axis=1).reshape(n_cfg * TILE, 1)
    in_use = jnp.arange(cap, dtype=jnp.int32)[None, None, :] < counts[:, :, None]
    target = jnp.where(in_use, dst_pos, -1)[:, :, None, :]
    own = jnp.arange(n_configs)[:, None] == jnp.arange(n_configs)[None, :]
    target = jnp.where(own[:, None, :, None], target, -1).reshape(n_configs, n_cfg, used)
    targets = jnp.pad(target, ((0, 0), (0, 0), (0, 8 - used)), constant_values=-1)
    targets = targets.reshape(n_configs, n_cfg * 8)
    vmem, anywhere = pl.BlockSpec(memory_space=pltpu.VMEM), pl.BlockSpec(memory_space=pl.ANY)
    smem = pl.BlockSpec(memory_space=pltpu.SMEM)
    dma, hops = pltpu.SemaphoreType.DMA, n_tp - 1
    arrived, base_kv, queries = pl.pallas_call(
        functools.partial(gather_kernel, n_cfg, n_tp),
        out_shape=(
            jax.ShapeDtypeStruct((n_cfg, TILE, HD), bf16),
            jax.ShapeDtypeStruct((holders, TILE, 2 * HD), bf16),
            jax.ShapeDtypeStruct((heads, 8, HD), f32),
        ),
        in_specs=[anywhere, smem, vmem, anywhere, anywhere, anywhere, vmem, vmem],
        out_specs=(vmem, vmem, vmem),
        scratch_shapes=[
            pltpu.VMEM((n_tp, seq, width), bf16),
            pltpu.VMEM((n_tp * width, 2 * HD), bf16),
            pltpu.VMEM(w_query.shape, bf16),
            pltpu.VMEM((holders, TILE, width), bf16),
            pltpu.VMEM((n_cfg, TILE, width), bf16),
            pltpu.VMEM((n_tp, TILE, width), bf16),
            pltpu.VMEM((TILE, HD), bf16),
            pltpu.VMEM((heads, TILE, HD), f32),
            pltpu.VMEM((n_cfg, TILE, HD), f32),
            pltpu.VMEM((n_cfg * TILE, 2 * seq), bf16),
            pltpu.VMEM((2 * seq, HD), bf16),
            pltpu.VMEM((n_cfg, TILE, HD), bf16),
            pltpu.VMEM((seq, 2 * HD), f32),
            pltpu.VMEM((seq, HD), f32),
            dma((4,)),
            dma((2, hops)),
            dma((2, hops)),
            dma((7,)),
            dma((7,)),
        ],
        compiler_params=pltpu.CompilerParams(
            collective_id=0, has_side_effects=True, vmem_limit_bytes=40 << 20
        ),
    )(
        pool[0],
        base_run,
        gains,
        w_key,
        w_value,
        w_query,
        picks,
        jnp.asarray(rope_tables(seq - 8, 8)),
    )
    return pl.pallas_call(
        attend_kernel,
        out_shape=(
            jax.ShapeDtypeStruct((n_configs, PROBE, heads * HD), bf16),
            jax.ShapeDtypeStruct((n_configs, seq, HD), bf16),
            jax.ShapeDtypeStruct((n_configs, seq, HD), bf16),
        ),
        in_specs=[vmem] * 5,
        out_specs=(vmem, vmem, vmem),
        compiler_params=pltpu.CompilerParams(vmem_limit_bytes=40 << 20),
    )(arrived, base_kv, queries, targets, jnp.asarray(rope_tables(0, seq)))


def solution(mesh):
    placed = (
        P("cfg", None, "tp"),
        P(),
        P(),
        P(None, "tp"),
        P(None, "tp"),
        P("cfg", "tp"),
        P(None, "cfg", None),
        P("cfg", None, None),
        P("cfg", None),
    )
    return jax.shard_map(
        functools.partial(body, mesh.shape["cfg"], mesh.shape["tp"]),
        mesh=mesh,
        in_specs=placed,
        out_specs=(P("cfg", None, "tp"), P("cfg", None, "tp"), P("cfg", None, "tp")),
        check_vma=False,
    )
```

time: 619 us -> 77.8 us (0.13)
  waiting for transfers between devices: 300 us -> 0 us
  blocking collectives: 246 us -> 0 us
  Pallas kernels: 0 us -> 67.7 us
  other arithmetic: 17.6 us -> 0.91 us
  matrix products: 15.3 us -> 0 us
  between operations: 14.9 us -> 1.39 us
  starting transfers between devices: 11.7 us -> 0 us
    psum x1 -> x0, blocking collectives: 246 us -> none  [body(): query_total = lax.psum(partial_value, 'cfg')]
    psum x1 -> x0, waiting for transfers between devices: 172 us -> none  [spread(): return lax.psum(kept, axis)]
    all_gather x1 -> x0, waiting for transfers between devices: 108 us -> none  [body(): widened = lax.all_gather(rows, 'tp', axis=1, tiled=True).astype(jnp.float32)]
    pallas_call x0 -> x2, Pallas kernels: none -> 67.7 us  [the longest x1 64.9 us: body(): pl.pallas_call(functools.partial(gather_kernel, n_cfg, n_tp), out_shape=(...]
    all_to_all x1 -> x0, waiting for transfers between devices: 20.7 us -> none  [body(): lax.all_to_all(picked, 'cfg', split_axis=0, concat_axis=1, tiled=True)]
    dot_general x6 -> x0, matrix products: 15.3 us -> none  [the longest x1 6.92 us: body(): values_acc = jnp.dot(normed, w_value, preferred_element_type=jnp.float32)]
    all_to_all x1 -> x0, starting transfers between devices: 11.6 us -> none  [body(): lax.all_to_all(picked, 'cfg', split_axis=0, concat_axis=1, tiled=True)]
    reduce_sum x2 -> x0, other arithmetic: 11.4 us -> none  [the longest x1 11.2 us: body(): squares = jnp.sum(widened * widened, axis=1)]
  transfers between devices with their start and end apart: 3 -> 0, of which waited for: 3 -> 0; matrix products, arithmetic and copies ran while one was open for 1% -> 0% of each run, Pallas kernels for 0% -> 0%
where the time goes in v1:
time: 77.8 us; the launch traced here: 77.4 us
  Pallas kernels  67.7 us (87%)
  local copies, waits for them, and re-layouts  7.41 us (10%)
  between operations  1.39 us (2%)
  other arithmetic  0.91 us (1%)
    pallas_call x1, Pallas kernels, body(): pl.pallas_call(functools.partial(gather_kernel, n_cfg, n_tp), out_shape=(...  64.9 us
    unnamed x18, local copies, waits for them, and re-layouts  6.74 us
    pallas_call x1, Pallas kernels, body(): pl.pallas_call(attend_kernel, out_shape=(jax.ShapeDtypeStruct((n_configs,...  2.73 us

profile of v1, /device:TPU:1, one launch (start us, length us, event | category | flops | bytes accessed | tf_op | source)
XLA Modules:
  0.0 77.4 jit_solution(8895882535911812817)
XLA Ops:
  0.6 0.8 %copy.24 = s32[192,1,2]{2,0,1:T(8,128)S(1)} copy(s32[192,1,2]{0,2,1:T(2,128)} %param.17) | data formatting | bytes 3072 | tf_op args[6]
  1.4 0.1 reshape.39
  1.5 0.1 pad_add_fusion
  1.6 0.3 reshape.44.picks
  1.9 0.7 reshape.42
  3.3 0.0 copy-start
  3.3 1.6 %copy-done = bf16[8192,128]{1,0:T(8,128)(2,1)S(1)} copy-done((bf16[8192,128]{1,0:T(8,128)(2,1)S(1)}, bf16[8192,128]{1,0:T(8,128)(2,1)}, u32[]{:S(2)}) %copy-start) | copy-done | bytes 2097176
  4.9 0.0 copy-start.1
  4.9 1.6 %copy-done.1 = bf16[8192,128]{1,0:T(8,128)(2,1)S(1)} copy-done((bf16[8192,128]{1,0:T(8,128)(2,1)S(1)}, bf16[8192,128]{1,0:T(8,128)(2,1)}, u32[]{:S(2)}) %copy-start.1) | copy-done | bytes 2097176
  6.5 0.0 copy-start.2
  6.5 1.0 %copy-done.2 = bf16[1,192,1024]{2,1,0:T(8,128)(2,1)S(1)} copy-done((bf16[1,192,1024]{2,1,0:T(8,128)(2,1)S(1)}, bf16[1,192,1024]{2,1,0:T(8,128)(2,1)}, u32[]{:S(2)}) %copy-start.2) | copy-done | bytes 393240
  7.5 0.0 copy-start.3
  7.5 0.9 %copy-done.3 = bf16[128,1024]{1,0:T(8,128)(2,1)S(1)} copy-done((bf16[128,1024]{1,0:T(8,128)(2,1)S(1)}, bf16[128,1024]{1,0:T(8,128)(2,1)}, u32[]{:S(2)}) %copy-start.3) | copy-done | bytes 262168
  8.4 0.7 copy-done.5
  9.1 64.9 %shard_map.130 = (bf16[64,16,128]{2,1,0:T(8,128)(2,1)S(1)}, bf16[12,16,256]{2,1,0:T(8,128)(2,1)S(1)}, f32[8,8,128]{2,1,0:T(8,128)S(1)}) custom-call(bf16[192,1024]{1,0:T(8,128)(2,1)S(1)} %bitcast.6, s32[1]{0:T(128)S(6)} %copy.28.base, f32[64,1,128]{2,1,0:T(1,128)S(1)} %bitcast.7, bf16[8192,128]{1,0:T(8,128)(2,1)S(1)} %copy-done, ...), custom_call_target="tpu_custom_call" | custom-call | tf_op jit(solution)/shard_map/pallas_call | solution.py:427
  74.1 0.0 copy-done.6
  74.1 0.0 copy-done.7
  74.2 0.1 broadcast_in_dim.36
  74.2 0.1 broadcast_in_dim.37
  74.3 0.1 broadcast_select_fusion
  74.4 0.1 copy.27
  74.5 0.1 reshape.41.targets
  74.6 0.0 copy-done.4
  74.7 2.7 %shard_map.131 = (bf16[3,4,1024]{2,1,0:T(4,128)(2,1)}, bf16[3,192,128]{2,1,0:T(8,128)(2,1)}, bf16[3,192,128]{2,1,0:T(8,128)(2,1)}) custom-call(bf16[64,16,128]{2,1,0:T(8,128)(2,1)S(1)} %get-tuple-element.6.arrived, bf16[12,16,256]{2,1,0:T(8,128)(2,1)S(1)} %get-tuple-element.7.base_kv, f32[8,8,128]{2,1,0:T(8,128)S(1)} %get-tuple-element.8.queries, ...), custom_call_target="tpu_custom_call" | custom-call | tf_op jit(solution)/shard_map/pallas_call | solution.py:470
  (10 shorter events, 0.1 us)
Async XLA Ops:
  3.3 1.6 %copy-start = (bf16[8192,128]{1,0:T(8,128)(2,1)S(1)}, bf16[8192,128]{1,0:T(8,128)(2,1)}, u32[]{:S(2)}) copy-start(bf16[8192,128]{1,0:T(8,128)(2,1)} %w_key.1) | copy-start | bytes 6291460
  4.9 1.6 %copy-start.1 = (bf16[8192,128]{1,0:T(8,128)(2,1)S(1)}, bf16[8192,128]{1,0:T(8,128)(2,1)}, u32[]{:S(2)}) copy-start(bf16[8192,128]{1,0:T(8,128)(2,1)} %w_value.1) | copy-start | bytes 6291460
  6.5 1.0 %copy-start.2 = (bf16[1,192,1024]{2,1,0:T(8,128)(2,1)S(1)}, bf16[1,192,1024]{2,1,0:T(8,128)(2,1)}, u32[]{:S(2)}) copy-start(bf16[1,192,1024]{2,1,0:T(8,128)(2,1)} %param.11) | copy-start | bytes 1179652
  7.5 0.9 %copy-start.3 = (bf16[128,1024]{1,0:T(8,128)(2,1)S(1)}, bf16[128,1024]{1,0:T(8,128)(2,1)}, u32[]{:S(2)}) copy-start(bf16[128,1024]{1,0:T(8,128)(2,1)} %w_query.1) | copy-start | bytes 786436
  8.4 0.7 copy-start.5
  9.1 65.0 %copy-start.6 = (s32[3,64,2]{1,2,0:T(2,128)S(1)}, s32[3,64,2]{1,2,0:T(2,128)}, u32[]{:S(2)}) copy-start(s32[3,64,2]{1,2,0:T(2,128)} %param.18) | copy-start | bytes 4612
  9.1 65.0 %copy-start.7 = (s32[3,64]{1,0:T(4,128)S(1)}, s32[3,64]{1,0:T(4,128)}, u32[]{:S(2)}) copy-start(s32[3,64]{1,0:T(4,128)} %param.19) | copy-start | bytes 2308
  9.1 65.5 %copy-start.4 = (f32[2,192,128]{2,1,0:T(8,128)S(1)}, f32[2,192,128]{2,1,0:T(8,128)}, u32[]{:S(2)}) copy-start(f32[2,192,128]{2,1,0:T(8,128)} %constant.11.clone.rope) | copy-start | bytes 589828

commit v2 on v1

--- a/solution.py
+++ b/solution.py
@@ -40,7 +40,7 @@
     return total
 
 
-def gather_kernel(
+def sweep_kernel(
     n_cfg,
     n_tp,
     pool,
@@ -49,25 +49,41 @@
     w_key,
     w_value,
     w_query,
-    picks,
-    rope,
-    arrived,
-    base_kv,
-    queries,
+    src_pos,
+    dst_pos,
+    counts,
+    rope_table,
+    attended,
+    keys,
+    values,
     rows,
     weights,
     wq,
+    gain_raw,
+    gain_wide,
+    src,
+    dst,
+    used,
+    rope,
     masked,
+    row_sums,
+    middle,
     landed,
     base_rows,
     block,
     part,
     parts,
+    queries,
+    base_kv,
     chosen,
+    placed,
+    uncovered,
     kv,
     outgoing,
+    arrived,
     acc,
     sums,
+    many,
     load_sem,
     ring_send,
     ring_recv,
@@ -79,21 +95,32 @@
     half_rows = seq // 2
     model = n_tp * width
     heads = queries.shape[0]
-    holders = seq // TILE
-    spacing = n_cfg // holders
-    is_holder = jnp.logical_and(lax.rem(cfg, spacing) == 0, cfg < holders * spacing)
-    my_tile = cfg // spacing
-    last_holder = (holders - 1) * spacing
+    group, tile = masked.shape[0], masked.shape[1]
+    rings = n_cfg // group
+    place, turn = lax.rem(cfg, group), cfg // group
+    holder = lax.rem(place, rings) * group + place
+    is_holder = cfg == holder
+    last_holder = (group - 1) % rings * group + group - 1
     owner_step = (n_cfg - 1) // (heads - 1)
     is_owner = jnp.logical_and(lax.rem(cfg, owner_step) == 0, cfg < heads * owner_step)
     my_head = cfg // owner_step
     per_plane = n_cfg // n_tp
 
     loads = [
-        pltpu.make_async_copy(pool, rows.at[tp], load_sem.at[0]),
-        pltpu.make_async_copy(w_key, weights.at[:, pl.ds(0, HD)], load_sem.at[1]),
-        pltpu.make_async_copy(w_value, weights.at[:, pl.ds(HD, HD)], load_sem.at[2]),
-        pltpu.make_async_copy(w_query, wq, load_sem.at[3]),
+        pltpu.make_async_copy(source, target, load_sem.at[i])
+        for i, (source, target) in enumerate(
+            (
+                (pool, rows.at[tp]),
+                (gain, gain_raw),
+                (w_key, weights.at[:, pl.ds(0, HD)]),
+                (w_value, weights.at[:, pl.ds(HD, HD)]),
+                (w_query, wq),
+                (src_pos, src),
+                (dst_pos, dst),
+                (counts, used),
+                (rope_table, rope),
+            )
+        )
     ]
     for load in loads:
         load.start()
@@ -113,9 +140,9 @@
         )
 
     loads[0].wait()
-    is_base = jnp.full((TILE, width), base[0], jnp.int32) == cfg
-    for j in range(holders):
-        mine = rows[tp, pl.ds(j * TILE, TILE), :].astype(f32)
+    is_base = jnp.full((tile, width), base[0], jnp.int32) == cfg
+    for j in range(group):
+        mine = rows[tp, pl.ds(j * tile, tile), :].astype(f32)
         masked[j] = jnp.where(is_base, mine, 0.0).astype(bf16)
     pl.semaphore_wait(barrier, n_cfg - 1 + n_tp - 1)
 
@@ -148,7 +175,8 @@
         )
 
     def gains(slot):
-        return jnp.concatenate([gain[slot * per_plane + k] for k in range(per_plane)], axis=1)
+        eight = gain_wide[slot]
+        return jnp.concatenate([eight[k : k + 1, :] for k in range(per_plane)], axis=1)
 
     def project(slot, part_no):
         piece = pl.ds(part_no * half_rows, half_rows)
@@ -180,38 +208,94 @@
         ring(0, unit).start()
         ring(1, unit).start()
 
-    for j in range(holders):
-
-        @pl.when(cfg != j * spacing)
-        def _():
-            to_cfg(masked.at[j], landed.at[cfg], 0, j * spacing).start()
-
-    @pl.when(is_holder)
-    def _():
-        landed[cfg] = masked[my_tile]
-
+    @pl.loop(1, group)
+    def _(i):
+        other = lax.rem(place + i, group)
+        to_cfg(masked.at[other], row_sums.at[place], 0, turn * group + other).start()
+
+    row_sums[place] = masked[place]
     acc[...] = jnp.zeros_like(acc)
     sums[...] = jnp.zeros_like(sums)
+    kv[...] = jnp.zeros_like(kv)
     for load in loads[1:]:
         load.wait()
+    for z in range(n_tp):
+        gain_wide[z] = gain_raw[...].astype(f32)[z * per_plane : (z + 1) * per_plane, :]
     project(tp, 0)
     project(tp, 1)
-    column = lax.broadcasted_iota(jnp.int32, (TILE * 4, 2 * seq), 1)
+
+    def base_meets():
+        settle(row_sums.at[pl.ds(0, group - 1)], recv.at[0])
+        total = row_sums[0].astype(f32)
+        for q in range(1, group):
+            total += row_sums[q].astype(f32)
+        middle[...] = total.astype(bf16)
+
+        @pl.when(jnp.logical_not(is_holder))
+        def _():
+            to_cfg(middle, landed.at[turn], 7, holder).start()
+
+        @pl.when(is_holder)
+        def _():
+            landed[turn] = middle[...]
+
+    padded = kv.shape[0] // 2
+    span_rows = TILE * 4
+    config = lax.broadcasted_iota(jnp.int32, (span_rows, src.shape[1]), 1)
+    row_no = lax.broadcasted_iota(jnp.int32, (padded, src.shape[1]), 0)
+    cap = src.shape[0]
+    n_configs = keys.shape[0]
+    asked = [(row_no == src[j : j + 1, :]).astype(f32).astype(bf16) for j in range(cap)]
+    is_key = lax.broadcasted_iota(jnp.int32, (span_rows, padded), 0) % TILE < 8
 
     @pl.loop(0, n_cfg // 4)
     def _(i):
-        span = pl.ds(pl.multiple_of(i * TILE * 4, TILE * 4), TILE * 4)
-        chosen[span, :] = (column == picks[span, :]).astype(f32).astype(bf16)
+        span = pl.ds(pl.multiple_of(i * span_rows, span_rows), span_rows)
+        slot = lax.broadcasted_iota(jnp.int32, (span_rows, src.shape[1]), 0)
+        target = i * 4 + lax.shift_right_logical(slot, 4)
+        slot = slot & 7
+        found = jnp.zeros((span_rows, padded), f32)
+        for j in range(cap):
+            wanted = jnp.zeros(slot.shape, f32)
+            for k in range(n_configs):
+                hit = jnp.logical_and(config == target * n_configs + k, slot == k * cap + j)
+                wanted = wanted + hit.astype(f32)
+            found += lax.dot_general(
+                wanted.astype(bf16),
+                asked[j],
+                (((1,), (1,)), ((), ())),
+                preferred_element_type=f32,
+            )
+        chosen[span, pl.ds(0, padded)] = jnp.where(is_key, found, 0.0).astype(bf16)
+        chosen[span, pl.ds(padded, padded)] = jnp.where(is_key, 0.0, found).astype(bf16)
+
+    slots = n_cfg * 8
+    source = lax.broadcasted_iota(jnp.int32, (n_cfg, slots), 0)
+    slot = lax.broadcasted_iota(jnp.int32, (n_cfg, slots), 1)
+    spread = (source == lax.shift_right_logical(slot, 3)).astype(f32).astype(bf16)
+    position = lax.broadcasted_iota(jnp.int32, (seq, slots), 0).astype(f32) + 1.0
+    slot_of = lax.broadcasted_iota(jnp.int32, (8, slots), 1) & 7
+    order = lax.broadcasted_iota(jnp.int32, (cap, n_cfg), 0)
+    for i in range(n_configs):
+        valid = order < used[i : i + 1, :]
+        goal = jnp.where(valid, dst[i] + 1, 0).astype(f32)
+        goal = jnp.concatenate([goal, jnp.zeros((8 - cap, n_cfg), f32)], axis=0)
+        wide = jnp.dot(goal.astype(bf16), spread, preferred_element_type=f32)
+        row_id = lax.broadcasted_iota(jnp.int32, (8, slots), 0)
+        mine = jnp.logical_and(slot_of == row_id + i * cap, row_id < cap)
+        goal = jnp.sum(jnp.where(mine, wide, 0.0), axis=0, keepdims=True)
+        onehot = (position == goal).astype(f32)
+        placed[pl.ds(i * seq, seq), :] = onehot.astype(bf16)
+        free = 1.0 - jnp.max(onehot, axis=1, keepdims=True)
+        uncovered[pl.ds(i * seq, seq), :] = jnp.broadcast_to(free, (seq, 2 * HD))
 
     def base_arrives():
         @pl.when(is_holder)
         def _():
-            settle(landed.at[pl.ds(0, n_cfg - 1)], recv.at[0])
-
-            def add(s, total):
-                return total + landed[s].astype(f32)
-
-            total = lax.fori_loop(0, n_cfg, add, jnp.zeros((TILE, width), f32))
+            settle(landed.at[pl.ds(0, rings - 1)], recv.at[7])
+            total = landed[0].astype(f32)
+            for y in range(1, rings):
+                total += landed[y].astype(f32)
             base_rows[tp] = total.astype(bf16)
 
             @pl.loop(1, n_tp)
@@ -250,15 +334,15 @@
                 return total, squares + lane_groups(wide * wide)
 
             total, squares = lax.fori_loop(
-                0, n_tp, add, (jnp.zeros((TILE, 2 * HD), f32), jnp.zeros((TILE, HD), f32))
+                0, n_tp, add, (jnp.zeros((tile, 2 * HD), f32), jnp.zeros((tile, HD), f32))
             )
             scale = lax.rsqrt(jnp.sum(squares, axis=1, keepdims=True) / model + EPSILON)
-            base_kv[my_tile] = (total * scale).astype(bf16)
+            base_kv[place] = (total * scale).astype(bf16)
 
             @pl.loop(1, n_cfg)
             def _(i):
                 to_cfg(
-                    base_kv.at[my_tile], base_kv.at[my_tile], 3, lax.rem(cfg + i, n_cfg)
+                    base_kv.at[place], base_kv.at[place], 3, lax.rem(cfg + i, n_cfg)
                 ).start()
 
     def query_parts():
@@ -266,13 +350,16 @@
         def _():
             settle(block, recv.at[2])
 
-        wide = block[...].astype(f32)
-        normed = (wide * gain[cfg]).astype(bf16)
+        wide = block[...].astype(f32)[tile - 8 :, :]
+        own_gain = gain_wide[cfg // per_plane]
+        pick = lax.broadcasted_iota(jnp.int32, own_gain.shape, 0) == lax.rem(cfg, per_plane)
+        own_gain = jnp.sum(jnp.where(pick, own_gain, 0.0), axis=0, keepdims=True)
+        normed = (wide * own_gain).astype(bf16)
         total = jnp.dot(normed, wq[...], preferred_element_type=f32)
         squares = wide * wide
         for h in range(heads):
-            part[h, pl.ds(0, 8), :] = total[8:, h * HD : (h + 1) * HD]
-            part[h, pl.ds(8, 8), :] = squares[8:, :]
+            part[h, pl.ds(0, 8), :] = total[:, h * HD : (h + 1) * HD]
+            part[h, pl.ds(8, 8), :] = squares
         for h in range(heads):
 
             @pl.when(cfg != h * owner_step)
@@ -293,7 +380,9 @@
 
             total = lax.fori_loop(0, n_cfg, add, jnp.zeros((TILE, HD), f32))
             scale = lax.rsqrt(jnp.sum(total[8:], axis=1, keepdims=True) / model + EPSILON)
-            queries[my_head] = rotate(total[:8] * scale, rope[0], rope[1])
+            queries[my_head] = rotate(
+                total[:8] * scale, rope[0, pl.ds(seq - 8, 8), :], rope[1, pl.ds(seq - 8, 8), :]
+            )
 
             @pl.loop(1, n_cfg)
             def _(i):
@@ -301,7 +390,7 @@
                     queries.at[my_head], queries.at[my_head], 5, lax.rem(cfg + i, n_cfg)
                 ).start()
 
-    beside = {1: base_arrives, 2: base_projects, 3: query_parts, 4: query_sums}
+    beside = {0: base_meets, 1: base_arrives, 2: base_projects, 3: query_parts, 4: query_sums}
     for unit in range(units):
         ring_step(unit)
         if unit in beside:
@@ -312,7 +401,7 @@
     scale = lax.rsqrt(jnp.sum(sums[...], axis=1, keepdims=True) / model + EPSILON)
     scaled = (acc[...] * scale).astype(bf16)
     kv[pl.ds(0, seq), :] = scaled[:, :HD]
-    kv[pl.ds(seq, seq), :] = scaled[:, HD:]
+    kv[pl.ds(padded, seq), :] = scaled[:, HD:]
     picked = jnp.dot(chosen[...], kv[...], preferred_element_type=f32).astype(bf16)
     outgoing[...] = picked.reshape(n_cfg, TILE, HD)
 
@@ -323,28 +412,27 @@
 
     arrived[cfg] = outgoing[cfg]
 
+    def both(condition, if_true, if_false):
+        pl.when(condition)(if_true)
+        pl.when(jnp.logical_not(condition))(if_false)
+
     for unit in range(units):
         for direction in (0, 1):
             ring(direction, unit).wait_send()
-
-    def both(condition, if_true, if_false):
-        pl.when(condition)(if_true)
-        pl.when(jnp.logical_not(condition))(if_false)
-
-    both(
-        is_holder,
-        lambda: settle(masked.at[pl.ds(0, holders - 1)], send.at[0]),
-        lambda: settle(masked, send.at[0]),
-    )
+    settle(masked.at[pl.ds(0, group - 1)], send.at[0])
+
+    @pl.when(jnp.logical_not(is_holder))
+    def _():
+        settle(middle, send.at[7])
 
     @pl.when(is_holder)
     def _():
         settle(base_rows.at[pl.ds(0, n_tp - 1)], send.at[1])
-        settle(landed.at[pl.ds(0, n_cfg - 1), :, pl.ds(0, 2 * HD)], send.at[3])
+        settle(many.at[pl.ds(0, n_cfg - 1), :, pl.ds(0, 2 * HD)], send.at[3])
 
     @pl.when(cfg == last_holder)
     def _():
-        settle(arrived.at[pl.ds(0, n_cfg - 1)], send.at[2])
+        settle(many.at[pl.ds(0, n_cfg - 1), :, pl.ds(0, HD)], send.at[2])
 
     both(
         is_owner,
@@ -353,7 +441,7 @@
     )
     both(
         is_holder,
-        lambda: settle(base_kv.at[pl.ds(0, holders - 1)], recv.at[3]),
+        lambda: settle(base_kv.at[pl.ds(0, group - 1)], recv.at[3]),
         lambda: settle(base_kv, recv.at[3]),
     )
     both(
@@ -367,30 +455,22 @@
         settle(arrived.at[pl.ds(0, n_cfg - 1)], send.at[5])
 
     settle(outgoing.at[pl.ds(0, n_cfg - 1)], send.at[6])
+    base_all = base_kv[...].astype(f32).reshape(seq, 2 * HD)
+    probes = queries[...].reshape(heads * 8, HD).astype(bf16)
+    probe_row = lax.broadcasted_iota(jnp.int32, (heads * 8, seq), 0) & 7
+    causal = lax.broadcasted_iota(jnp.int32, (heads * 8, seq), 1) <= seq - 8 + probe_row
     settle(arrived.at[pl.ds(0, n_cfg - 1)], recv.at[6])
 
-
-def attend_kernel(arrived, base_kv, queries, targets, rope, attended, keys, values):
-    n_configs, seq = keys.shape[0], keys.shape[1]
-    heads = queries.shape[0]
     spliced = arrived[...].astype(f32)
-    slots = spliced.shape[0] * 8
-    rows = jnp.concatenate(
+    taken_rows = jnp.concatenate(
         [spliced[:, :8, :].reshape(slots, HD), spliced[:, 8:, :].reshape(slots, HD)], axis=1
     ).astype(bf16)
-    base = base_kv[...].reshape(seq, 2 * HD).astype(f32)
-    probes = queries[...].reshape(heads * 8, HD).astype(bf16)
-    position = lax.broadcasted_iota(jnp.int32, (seq, slots), 0)
-    probe_row = lax.broadcasted_iota(jnp.int32, (heads * 8, seq), 0)
-    causal = lax.broadcasted_iota(jnp.int32, (heads * 8, seq), 1) <= seq - 8 + lax.rem(probe_row, 8)
-    cosine, sine = rope[0], rope[1]
     for i in range(n_configs):
-        onehot = (position == targets[pl.ds(i, 1), :]).astype(f32)
-        covered = jnp.max(onehot, axis=1, keepdims=True)
-        taken = jnp.dot(onehot.astype(bf16), rows, preferred_element_type=f32)
-        both = jnp.where(covered > 0.0, taken, base)
-        key = rotate(both[:, :HD], cosine, sine).astype(bf16)
-        value = both[:, HD:].astype(bf16)
+        span = pl.ds(i * seq, seq)
+        taken = jnp.dot(placed[span, :], taken_rows, preferred_element_type=f32)
+        mixed = jnp.where(uncovered[span, :] > 0.5, base_all, taken)
+        key = rotate(mixed[:, :HD], rope[0], rope[1]).astype(bf16)
+        value = mixed[:, HD:].astype(bf16)
         keys[i] = key
         values[i] = value
         scores = lax.dot_general(
@@ -408,76 +488,72 @@
 def body(n_cfg, n_tp, pool, base_run, gain, w_key, w_value, w_query, src_pos, dst_pos, counts):
     seq, width = pool.shape[1], pool.shape[2]
     n_configs, cap = dst_pos.shape[0], dst_pos.shape[2]
-    used = n_configs * cap
     heads = w_query.shape[1] // HD
-    holders = seq // TILE
-    gains = gain.astype(f32).reshape(n_cfg, 1, HD)
-    wanted = src_pos.reshape(n_cfg, used)
-    wanted = jnp.pad(wanted, ((0, 0), (0, 8 - used)), constant_values=-2 * seq)
-    picks = jnp.concatenate([wanted, wanted + seq], axis=1).reshape(n_cfg * TILE, 1)
-    in_use = jnp.arange(cap, dtype=jnp.int32)[None, None, :] < counts[:, :, None]
-    target = jnp.where(in_use, dst_pos, -1)[:, :, None, :]
-    own = jnp.arange(n_configs)[:, None] == jnp.arange(n_configs)[None, :]
-    target = jnp.where(own[:, None, :, None], target, -1).reshape(n_configs, n_cfg, used)
-    targets = jnp.pad(target, ((0, 0), (0, 0), (0, 8 - used)), constant_values=-1)
-    targets = targets.reshape(n_configs, n_cfg * 8)
+    group = 1 << (n_cfg.bit_length() // 2)
+    tile = seq // group
+    padded = -(-seq // HD) * HD
     vmem, anywhere = pl.BlockSpec(memory_space=pltpu.VMEM), pl.BlockSpec(memory_space=pl.ANY)
     smem = pl.BlockSpec(memory_space=pltpu.SMEM)
     dma, hops = pltpu.SemaphoreType.DMA, n_tp - 1
-    arrived, base_kv, queries = pl.pallas_call(
-        functools.partial(gather_kernel, n_cfg, n_tp),
+    return pl.pallas_call(
+        functools.partial(sweep_kernel, n_cfg, n_tp),
         out_shape=(
-            jax.ShapeDtypeStruct((n_cfg, TILE, HD), bf16),
-            jax.ShapeDtypeStruct((holders, TILE, 2 * HD), bf16),
-            jax.ShapeDtypeStruct((heads, 8, HD), f32),
+            jax.ShapeDtypeStruct((n_configs, PROBE, heads * HD), bf16),
+            jax.ShapeDtypeStruct((n_configs, seq, HD), bf16),
+            jax.ShapeDtypeStruct((n_configs, seq, HD), bf16),
         ),
-        in_specs=[anywhere, smem, vmem, anywhere, anywhere, anywhere, vmem, vmem],
+        in_specs=[anywhere, smem] + [anywhere] * 8,
         out_specs=(vmem, vmem, vmem),
         scratch_shapes=[
             pltpu.VMEM((n_tp, seq, width), bf16),
             pltpu.VMEM((n_tp * width, 2 * HD), bf16),
             pltpu.VMEM(w_query.shape, bf16),
-            pltpu.VMEM((holders, TILE, width), bf16),
-            pltpu.VMEM((n_cfg, TILE, width), bf16),
-            pltpu.VMEM((n_tp, TILE, width), bf16),
-            pltpu.VMEM((TILE, HD), bf16),
+            pltpu.VMEM((n_cfg, HD), bf16),
+            pltpu.VMEM((n_tp, n_cfg // n_tp, HD), f32),
+            pltpu.VMEM((cap, n_configs * n_cfg), jnp.int32),
+            pltpu.VMEM((n_configs, cap, n_cfg), jnp.int32),
+            pltpu.VMEM((n_configs, n_cfg), jnp.int32),
+            pltpu.VMEM((2, seq, HD), f32),
+            pltpu.VMEM((group, tile, width), bf16),
+            pltpu.VMEM((group, tile, width), bf16),
+            pltpu.VMEM((tile, width), bf16),
+            pltpu.VMEM((n_cfg // group, tile, width), bf16),
+            pltpu.VMEM((n_tp, tile, width), bf16),
+            pltpu.VMEM((tile, HD), bf16),
             pltpu.VMEM((heads, TILE, HD), f32),
             pltpu.VMEM((n_cfg, TILE, HD), f32),
-            pltpu.VMEM((n_cfg * TILE, 2 * seq), bf16),
-            pltpu.VMEM((2 * seq, HD), bf16),
+            pltpu.VMEM((heads, 8, HD), f32),
+            pltpu.VMEM((group, tile, 2 * HD), bf16),
+            pltpu.VMEM((n_cfg * TILE, 2 * padded), bf16),
+            pltpu.VMEM((n_configs * seq, n_cfg * 8), bf16),
+            pltpu.VMEM((n_configs * seq, 2 * HD), f32),
+            pltpu.VMEM((2 * padded, HD), bf16),
+            pltpu.VMEM((n_cfg, TILE, HD), bf16),
             pltpu.VMEM((n_cfg, TILE, HD), bf16),
             pltpu.VMEM((seq, 2 * HD), f32),
             pltpu.VMEM((seq, HD), f32),
-            dma((4,)),
+            pltpu.VMEM((n_cfg, tile, 2 * HD), bf16),
+            dma((9,)),
             dma((2, hops)),
             dma((2, hops)),
-            dma((7,)),
-            dma((7,)),
+            dma((8,)),
+            dma((8,)),
         ],
         compiler_params=pltpu.CompilerParams(
-            collective_id=0, has_side_effects=True, vmem_limit_bytes=40 << 20
+            collective_id=0, has_side_effects=True, vmem_limit_bytes=60 << 20
         ),
     )(
         pool[0],
         base_run,
-        gains,
+        gain.reshape(n_cfg, HD),
         w_key,
         w_value,
         w_query,
-        picks,
-        jnp.asarray(rope_tables(seq - 8, 8)),
+        jnp.transpose(src_pos[:, 0, :], (1, 0)),
+        jnp.transpose(dst_pos, (0, 2, 1)),
+        counts,
+        jnp.asarray(rope_tables(0, seq)),
     )
-    return pl.pallas_call(
-        attend_kernel,
-        out_shape=(
-            jax.ShapeDtypeStruct((n_configs, PROBE, heads * HD), bf16),
-            jax.ShapeDtypeStruct((n_configs, seq, HD), bf16),
-            jax.ShapeDtypeStruct((n_configs, seq, HD), bf16),
-        ),
-        in_specs=[vmem] * 5,
-        out_specs=(vmem, vmem, vmem),
-        compiler_params=pltpu.CompilerParams(vmem_limit_bytes=40 << 20),
-    )(arrived, base_kv, queries, targets, jnp.asarray(rope_tables(0, seq)))
 
 
 def solution(mesh):

time: 77.8 us -> 76 us (0.977)
  local copies, waits for them, and re-layouts: 7.41 us -> 4.51 us
  Pallas kernels: 67.7 us -> 70 us
  other arithmetic: 0.91 us -> 0 us
    pallas_call x2 -> x1, Pallas kernels: 67.7 us -> 70 us  [body(): pl.pallas_call(functools.partial(sweep_kernel, n_cfg, n_tp), out_shape=(j...]
    unnamed x18 -> x3, local copies, waits for them, and re-layouts: 6.74 us -> 4.51 us
where the time goes in v2:
time: 76 us; the launch traced here: 75.8 us
  Pallas kernels  70 us (92%)
  local copies, waits for them, and re-layouts  4.51 us (6%)
  between operations  1.29 us (2%)
    pallas_call x1, Pallas kernels, body(): pl.pallas_call(functools.partial(sweep_kernel, n_cfg, n_tp), out_shape=(j...  70 us
    unnamed x3, local copies, waits for them, and re-layouts  4.51 us

profile of v2, /device:TPU:1, one launch (start us, length us, event | category | flops | bytes accessed | tf_op | source)
XLA Modules:
  0.0 75.8 jit_solution(11490827822204062180)
XLA Ops:
  1.3 70.0 %shard_map.121 = (bf16[3,4,1024]{2,1,0:T(4,128)(2,1)}, bf16[3,192,128]{2,1,0:T(8,128)(2,1)}, bf16[3,192,128]{2,1,0:T(8,128)(2,1)}) custom-call(bf16[192,1024]{1,0:T(8,128)(2,1)} %bitcast.6, s32[1]{0:T(128)S(6)} %copy.16.base, bf16[64,128]{1,0:T(8,128)(2,1)} %bitcast.7, bf16[8192,128]{1,0:T(8,128)(2,1)} %w_key.1, bf16[8192,128]{1,0:T(8,128)(2,1)} %w_value.1, ...), custom_call_target="tpu_custom_call" | custom-call | tf_op jit(solution)/shard_map/pallas_call | solution.py:498
  71.3 1.4 %copy.17 = bf16[3,4,1024]{2,1,0:T(4,128)(2,1)} copy(bf16[3,4,1024]{2,1,0:T(4,128)(2,1)} %get-tuple-element.6) | data formatting | bytes 49152
  72.6 1.6 %copy.18 = bf16[3,192,128]{2,1,0:T(8,128)(2,1)} copy(bf16[3,192,128]{2,1,0:T(8,128)(2,1)} %get-tuple-element.7) | data formatting | bytes 294912
  74.2 1.6 %copy.19 = bf16[3,192,128]{2,1,0:T(8,128)(2,1)} copy(bf16[3,192,128]{2,1,0:T(8,128)(2,1)} %get-tuple-element.8) | data formatting | bytes 294912

commit v3 on v2

--- a/solution.py
+++ b/solution.py
@@ -44,18 +44,20 @@
     n_cfg,
     n_tp,
     pool,
-    base,
+    base_run,
     gain,
     w_key,
     w_value,
     w_query,
     src_pos,
+    rope_table,
     dst_pos,
     counts,
-    rope_table,
-    attended,
-    keys,
-    values,
+    arrived,
+    base_kv,
+    queries,
+    splices,
+    base,
     rows,
     weights,
     wq,
@@ -65,25 +67,24 @@
     dst,
     used,
     rope,
+    placed,
     masked,
     row_sums,
     middle,
     landed,
     base_rows,
+    probe,
+    probes_met,
     block,
     part,
     parts,
-    queries,
-    base_kv,
+    my_queries,
+    my_base_kv,
     chosen,
-    placed,
-    uncovered,
     kv,
     outgoing,
-    arrived,
     acc,
     sums,
-    many,
     load_sem,
     ring_send,
     ring_recv,
@@ -100,38 +101,51 @@
     place, turn = lax.rem(cfg, group), cfg // group
     holder = lax.rem(place, rings) * group + place
     is_holder = cfg == holder
-    last_holder = (group - 1) % rings * group + group - 1
-    owner_step = (n_cfg - 1) // (heads - 1)
-    is_owner = jnp.logical_and(lax.rem(cfg, owner_step) == 0, cfg < heads * owner_step)
-    my_head = cfg // owner_step
+
+    def owner(head):
+        return (head + rings // 2) % rings * group + head
+
+    is_owner = jnp.logical_and(turn == lax.rem(place + rings // 2, rings), place < heads)
+    my_head = lax.rem(place, heads)
     per_plane = n_cfg // n_tp
+    makes_block = cfg // per_plane == tp
 
     loads = [
         pltpu.make_async_copy(source, target, load_sem.at[i])
         for i, (source, target) in enumerate(
             (
                 (pool, rows.at[tp]),
+                (base_run, base),
                 (gain, gain_raw),
                 (w_key, weights.at[:, pl.ds(0, HD)]),
                 (w_value, weights.at[:, pl.ds(HD, HD)]),
                 (w_query, wq),
                 (src_pos, src),
+                (rope_table, rope),
                 (dst_pos, dst),
                 (counts, used),
-                (rope_table, rope),
             )
         )
     ]
     for load in loads:
         load.start()
 
+    def outward(i, size):
+        step = lax.div(i + 1, 2)
+        return lax.rem(size // 2 + jnp.where(lax.rem(i, 2) == 0, step, size - step), size)
+
+    def peer(i):
+        across = lax.rem(i, group)
+        y = lax.rem(turn + outward(lax.div(i, group), rings), rings)
+        x = lax.rem(lax.div(place, 2) + outward(lax.div(across, 2), group // 2), group // 2)
+        core = lax.rem(place + 1 - lax.rem(across, 2), 2)
+        return y * group + x * 2 + core
+
     barrier = pltpu.get_barrier_semaphore()
 
-    @pl.loop(1, n_cfg)
+    @pl.loop(0, n_cfg - 1)
     def _(i):
-        pl.semaphore_signal(
-            barrier, inc=1, device_id={"cfg": lax.rem(cfg + i, n_cfg)}, device_id_type=MESH
-        )
+        pl.semaphore_signal(barrier, inc=1, device_id={"cfg": peer(i)}, device_id_type=MESH)
 
     @pl.loop(1, n_tp)
     def _(i):
@@ -140,10 +154,17 @@
         )
 
     loads[0].wait()
+    loads[1].wait()
     is_base = jnp.full((tile, width), base[0], jnp.int32) == cfg
     for j in range(group):
         mine = rows[tp, pl.ds(j * tile, tile), :].astype(f32)
         masked[j] = jnp.where(is_base, mine, 0.0).astype(bf16)
+    mine = rows[tp, pl.ds(seq - TILE, TILE), :].astype(f32)
+    probe[...] = jnp.where(is_base[:TILE, :], mine, 0.0).astype(bf16)
+    padded = kv.shape[0] // 2
+    cap = src.shape[0]
+    n_configs = src.shape[1] // n_cfg
+
     pl.semaphore_wait(barrier, n_cfg - 1 + n_tp - 1)
 
     def to_cfg(src, dst, which, target):
@@ -178,8 +199,8 @@
         eight = gain_wide[slot]
         return jnp.concatenate([eight[k : k + 1, :] for k in range(per_plane)], axis=1)
 
-    def project(slot, part_no):
-        piece = pl.ds(part_no * half_rows, half_rows)
+    def project(slot, part_no, parts_at_once=1):
+        piece = pl.ds(part_no * half_rows, half_rows * parts_at_once)
         wide = rows[slot, piece, :].astype(f32)
         sums[piece, :] += lane_groups(wide * wide)
         normed = (wide * gains(slot)).astype(bf16)
@@ -188,7 +209,7 @@
 
     units = n_tp - 1
 
-    def ring_step(unit):
+    def ring_arrives(unit):
         for direction in (0, 1):
             sign = 1 if direction == 0 else -1
             hop = unit // 2 + 1
@@ -198,15 +219,33 @@
             pltpu.make_async_copy(piece, piece, ring_recv.at[direction, unit]).wait()
             if unit + 2 < units:
                 ring(direction, unit + 2).start()
+
+    def ring_projects(unit):
+        if unit == units - 1:
+            project(lax.rem(tp + n_tp // 2, n_tp), 0, 2)
+            return
         for direction in (0, 1):
             sign = 1 if direction == 0 else -1
             hop = unit // 2 + 1
             part_no = unit % 2 if direction == 0 else 1 - unit % 2
             project(lax.rem(tp - sign * hop + n_tp, n_tp), part_no)
 
+    for k in range(per_plane):
+
+        @pl.when(cfg != tp * per_plane + k)
+        def _():
+            to_cfg(
+                probe.at[:, pl.ds(k * HD, HD)], probes_met.at[cfg], 2, tp * per_plane + k
+            ).start()
+
     for unit in range(min(2, units)):
         ring(0, unit).start()
         ring(1, unit).start()
+
+    @pl.when(makes_block)
+    def _():
+        lanes = pl.ds(pl.multiple_of(lax.rem(cfg, per_plane) * HD, HD), HD)
+        probes_met[cfg] = probe[:, lanes]
 
     @pl.loop(1, group)
     def _(i):
@@ -217,34 +256,11 @@
     acc[...] = jnp.zeros_like(acc)
     sums[...] = jnp.zeros_like(sums)
     kv[...] = jnp.zeros_like(kv)
-    for load in loads[1:]:
+    for load in loads[2:]:
         load.wait()
-    for z in range(n_tp):
-        gain_wide[z] = gain_raw[...].astype(f32)[z * per_plane : (z + 1) * per_plane, :]
-    project(tp, 0)
-    project(tp, 1)
-
-    def base_meets():
-        settle(row_sums.at[pl.ds(0, group - 1)], recv.at[0])
-        total = row_sums[0].astype(f32)
-        for q in range(1, group):
-            total += row_sums[q].astype(f32)
-        middle[...] = total.astype(bf16)
-
-        @pl.when(jnp.logical_not(is_holder))
-        def _():
-            to_cfg(middle, landed.at[turn], 7, holder).start()
-
-        @pl.when(is_holder)
-        def _():
-            landed[turn] = middle[...]
-
-    padded = kv.shape[0] // 2
     span_rows = TILE * 4
     config = lax.broadcasted_iota(jnp.int32, (span_rows, src.shape[1]), 1)
     row_no = lax.broadcasted_iota(jnp.int32, (padded, src.shape[1]), 0)
-    cap = src.shape[0]
-    n_configs = keys.shape[0]
     asked = [(row_no == src[j : j + 1, :]).astype(f32).astype(bf16) for j in range(cap)]
     is_key = lax.broadcasted_iota(jnp.int32, (span_rows, padded), 0) % TILE < 8
 
@@ -269,25 +285,70 @@
         chosen[span, pl.ds(0, padded)] = jnp.where(is_key, found, 0.0).astype(bf16)
         chosen[span, pl.ds(padded, padded)] = jnp.where(is_key, 0.0, found).astype(bf16)
 
-    slots = n_cfg * 8
-    source = lax.broadcasted_iota(jnp.int32, (n_cfg, slots), 0)
-    slot = lax.broadcasted_iota(jnp.int32, (n_cfg, slots), 1)
-    spread = (source == lax.shift_right_logical(slot, 3)).astype(f32).astype(bf16)
-    position = lax.broadcasted_iota(jnp.int32, (seq, slots), 0).astype(f32) + 1.0
-    slot_of = lax.broadcasted_iota(jnp.int32, (8, slots), 1) & 7
-    order = lax.broadcasted_iota(jnp.int32, (cap, n_cfg), 0)
-    for i in range(n_configs):
-        valid = order < used[i : i + 1, :]
-        goal = jnp.where(valid, dst[i] + 1, 0).astype(f32)
-        goal = jnp.concatenate([goal, jnp.zeros((8 - cap, n_cfg), f32)], axis=0)
-        wide = jnp.dot(goal.astype(bf16), spread, preferred_element_type=f32)
+    for z in range(n_tp):
+        gain_wide[z] = gain_raw[...].astype(f32)[z * per_plane : (z + 1) * per_plane, :]
+    project(tp, 0, 2)
+
+    def probes_meet():
+        @pl.when(makes_block)
+        def _():
+            settle(probes_met.at[pl.ds(0, n_cfg - 1)], recv.at[2])
+
+            def add(source, total):
+                return total + probes_met[source].astype(f32)
+
+            total = lax.fori_loop(0, n_cfg, add, jnp.zeros((TILE, HD), f32))
+            block[...] = total.astype(bf16)
+
+            @pl.loop(1, n_tp)
+            def _(i):
+                pltpu.make_async_remote_copy(
+                    src_ref=block,
+                    dst_ref=block,
+                    send_sem=send.at[8],
+                    recv_sem=recv.at[8],
+                    device_id={"tp": lax.rem(tp + i, n_tp)},
+                    device_id_type=MESH,
+                ).start()
+
+    def base_meets():
+        settle(row_sums.at[pl.ds(0, group - 1)], recv.at[0])
+        total = row_sums[0].astype(f32)
+        for q in range(1, group):
+            total += row_sums[q].astype(f32)
+        middle[...] = total.astype(bf16)
+
+        @pl.when(jnp.logical_not(is_holder))
+        def _():
+            to_cfg(middle, landed.at[turn], 7, holder).start()
+
+        @pl.when(is_holder)
+        def _():
+            landed[turn] = middle[...]
+
+    def place_slots():
+        slots = n_cfg * 8
+        source = lax.broadcasted_iota(jnp.int32, (n_cfg, slots), 0)
+        slot = lax.broadcasted_iota(jnp.int32, (n_cfg, slots), 1)
+        spread = (source == lax.shift_right_logical(slot, 3)).astype(f32).astype(bf16)
+        position = lax.broadcasted_iota(jnp.int32, (seq, slots), 0).astype(f32) + 1.0
+        slot_of = lax.broadcasted_iota(jnp.int32, (8, slots), 1) & 7
         row_id = lax.broadcasted_iota(jnp.int32, (8, slots), 0)
-        mine = jnp.logical_and(slot_of == row_id + i * cap, row_id < cap)
-        goal = jnp.sum(jnp.where(mine, wide, 0.0), axis=0, keepdims=True)
-        onehot = (position == goal).astype(f32)
-        placed[pl.ds(i * seq, seq), :] = onehot.astype(bf16)
-        free = 1.0 - jnp.max(onehot, axis=1, keepdims=True)
-        uncovered[pl.ds(i * seq, seq), :] = jnp.broadcast_to(free, (seq, 2 * HD))
+        order = lax.broadcasted_iota(jnp.int32, (cap, n_cfg), 0)
+        down = lax.broadcasted_iota(jnp.int32, (seq, padded), 0)
+        diagonal = (down == lax.broadcasted_iota(jnp.int32, (seq, padded), 1)).astype(f32)
+        for i in range(n_configs):
+            valid = order < used[i : i + 1, :]
+            goal = jnp.where(valid, dst[i] + 1, 0).astype(f32)
+            goal = jnp.concatenate([goal, jnp.zeros((8 - cap, n_cfg), f32)], axis=0)
+            wide = jnp.dot(goal.astype(bf16), spread, preferred_element_type=f32)
+            mine = jnp.logical_and(slot_of == row_id + i * cap, row_id < cap)
+            goal = jnp.sum(jnp.where(mine, wide, 0.0), axis=0, keepdims=True)
+            onehot = (position == goal).astype(f32)
+            free = 1.0 - jnp.max(onehot, axis=1, keepdims=True)
+            placed[pl.ds(i * seq, seq), pl.ds(0, slots)] = onehot.astype(bf16)
+            placed[pl.ds(i * seq, seq), pl.ds(slots, padded)] = (diagonal * free).astype(bf16)
+        pltpu.make_async_copy(placed, splices, load_sem.at[3]).start()
 
     def base_arrives():
         @pl.when(is_holder)
@@ -314,17 +375,6 @@
         def _():
             settle(base_rows.at[pl.ds(0, n_tp - 1)], recv.at[1])
 
-            @pl.when(cfg == last_holder)
-            def _():
-                @pl.loop(1, n_cfg)
-                def _(i):
-                    target = lax.rem(cfg + i, n_cfg)
-                    lanes = pl.ds(pl.multiple_of(lax.rem(target, per_plane) * HD, HD), HD)
-                    to_cfg(base_rows.at[target // per_plane, :, lanes], block, 2, target).start()
-
-                lanes = pl.ds(pl.multiple_of(lax.rem(cfg, per_plane) * HD, HD), HD)
-                block[...] = base_rows[cfg // per_plane, :, lanes]
-
             def add(z, state):
                 total, squares = state
                 wide = base_rows[z].astype(f32)
@@ -337,20 +387,31 @@
                 0, n_tp, add, (jnp.zeros((tile, 2 * HD), f32), jnp.zeros((tile, HD), f32))
             )
             scale = lax.rsqrt(jnp.sum(squares, axis=1, keepdims=True) / model + EPSILON)
-            base_kv[place] = (total * scale).astype(bf16)
-
-            @pl.loop(1, n_cfg)
+            my_base_kv[...] = (total * scale).astype(bf16)
+
+            @pl.loop(0, rings - 1)
             def _(i):
-                to_cfg(
-                    base_kv.at[place], base_kv.at[place], 3, lax.rem(cfg + i, n_cfg)
-                ).start()
+                other = lax.rem(turn + outward(i, rings), rings)
+                to_cfg(my_base_kv, my_base_kv, 3, other * group + place).start()
+
+    def base_spreads():
+        @pl.when(jnp.logical_not(is_holder))
+        def _():
+            settle(my_base_kv, recv.at[3])
+
+        @pl.loop(1, group)
+        def _(i):
+            other = lax.rem(place + i, group)
+            to_cfg(my_base_kv, base_kv.at[place], 9, turn * group + other).start()
+
+        pltpu.make_async_copy(my_base_kv, base_kv.at[place], load_sem.at[0]).start()
 
     def query_parts():
-        @pl.when(cfg != last_holder)
-        def _():
-            settle(block, recv.at[2])
-
-        wide = block[...].astype(f32)[tile - 8 :, :]
+        @pl.when(jnp.logical_not(makes_block))
+        def _():
+            settle(block, recv.at[8])
+
+        wide = block[...].astype(f32)[TILE - 8 :, :]
         own_gain = gain_wide[cfg // per_plane]
         pick = lax.broadcasted_iota(jnp.int32, own_gain.shape, 0) == lax.rem(cfg, per_plane)
         own_gain = jnp.sum(jnp.where(pick, own_gain, 0.0), axis=0, keepdims=True)
@@ -362,9 +423,9 @@
             part[h, pl.ds(8, 8), :] = squares
         for h in range(heads):
 
-            @pl.when(cfg != h * owner_step)
+            @pl.when(cfg != owner(h))
             def _():
-                to_cfg(part.at[h], parts.at[cfg], 4, h * owner_step).start()
+                to_cfg(part.at[h], parts.at[cfg], 4, owner(h)).start()
 
         @pl.when(is_owner)
         def _():
@@ -380,23 +441,32 @@
 
             total = lax.fori_loop(0, n_cfg, add, jnp.zeros((TILE, HD), f32))
             scale = lax.rsqrt(jnp.sum(total[8:], axis=1, keepdims=True) / model + EPSILON)
-            queries[my_head] = rotate(
+            my_queries[...] = rotate(
                 total[:8] * scale, rope[0, pl.ds(seq - 8, 8), :], rope[1, pl.ds(seq - 8, 8), :]
             )
 
-            @pl.loop(1, n_cfg)
+            pltpu.make_async_copy(my_queries, queries.at[my_head], load_sem.at[1]).start()
+
+            @pl.loop(0, n_cfg - 1)
             def _(i):
-                to_cfg(
-                    queries.at[my_head], queries.at[my_head], 5, lax.rem(cfg + i, n_cfg)
-                ).start()
-
-    beside = {0: base_meets, 1: base_arrives, 2: base_projects, 3: query_parts, 4: query_sums}
-    for unit in range(units):
-        ring_step(unit)
-        if unit in beside:
-            beside.pop(unit)()
-    for unit in sorted(beside):
-        beside[unit]()
+                to_cfg(my_queries, queries.at[my_head], 5, peer(i)).start()
+
+    beside = [
+        (probes_meet, base_meets),
+        (base_arrives, query_parts),
+        (place_slots,),
+        (base_projects,),
+        (query_sums,),
+        (base_spreads,),
+    ]
+    for unit in range(max(units, len(beside))):
+        if unit < units:
+            ring_arrives(unit)
+        if unit < len(beside):
+            for stage in beside[unit]:
+                stage()
+        if unit < units:
+            ring_projects(unit)
 
     scale = lax.rsqrt(jnp.sum(sums[...], axis=1, keepdims=True) / model + EPSILON)
     scaled = (acc[...] * scale).astype(bf16)
@@ -405,12 +475,13 @@
     picked = jnp.dot(chosen[...], kv[...], preferred_element_type=f32).astype(bf16)
     outgoing[...] = picked.reshape(n_cfg, TILE, HD)
 
-    @pl.loop(1, n_cfg)
+    @pl.loop(0, n_cfg - 1)
     def _(i):
-        target = lax.rem(cfg + i, n_cfg)
+        target = peer(i)
         to_cfg(outgoing.at[target], arrived.at[cfg], 6, target).start()
 
-    arrived[cfg] = outgoing[cfg]
+    own = pltpu.make_async_copy(outgoing.at[cfg], arrived.at[cfg], load_sem.at[2])
+    own.start()
 
     def both(condition, if_true, if_false):
         pl.when(condition)(if_true)
@@ -428,22 +499,25 @@
     @pl.when(is_holder)
     def _():
         settle(base_rows.at[pl.ds(0, n_tp - 1)], send.at[1])
-        settle(many.at[pl.ds(0, n_cfg - 1), :, pl.ds(0, 2 * HD)], send.at[3])
-
-    @pl.when(cfg == last_holder)
+        settle(base_kv.at[pl.ds(0, rings - 1)], send.at[3])
+
+    both(
+        makes_block,
+        lambda: settle(probes_met.at[pl.ds(0, per_plane - 1)], send.at[2]),
+        lambda: settle(probes_met.at[pl.ds(0, per_plane)], send.at[2]),
+    )
+
+    @pl.when(makes_block)
     def _():
-        settle(many.at[pl.ds(0, n_cfg - 1), :, pl.ds(0, HD)], send.at[2])
+        settle(probes_met.at[pl.ds(0, n_tp - 1)], send.at[8])
 
     both(
         is_owner,
         lambda: settle(part.at[pl.ds(0, heads - 1)], send.at[4]),
         lambda: settle(part, send.at[4]),
     )
-    both(
-        is_holder,
-        lambda: settle(base_kv.at[pl.ds(0, group - 1)], recv.at[3]),
-        lambda: settle(base_kv, recv.at[3]),
-    )
+    settle(base_kv.at[pl.ds(0, group - 1)], send.at[9])
+    settle(base_kv.at[pl.ds(0, group - 1)], recv.at[9])
     both(
         is_owner,
         lambda: settle(queries.at[pl.ds(0, heads - 1)], recv.at[5]),
@@ -455,20 +529,65 @@
         settle(arrived.at[pl.ds(0, n_cfg - 1)], send.at[5])
 
     settle(outgoing.at[pl.ds(0, n_cfg - 1)], send.at[6])
-    base_all = base_kv[...].astype(f32).reshape(seq, 2 * HD)
-    probes = queries[...].reshape(heads * 8, HD).astype(bf16)
+    settle(arrived.at[pl.ds(0, n_cfg - 1)], recv.at[6])
+    own.wait()
+    pltpu.make_async_copy(placed, splices, load_sem.at[3]).wait()
+
+    pltpu.make_async_copy(my_base_kv, base_kv.at[place], load_sem.at[0]).wait()
+
+    @pl.when(is_owner)
+    def _():
+        pltpu.make_async_copy(my_queries, queries.at[my_head], load_sem.at[1]).wait()
+
+
+def attend_kernel(
+    arrived_in,
+    base_in,
+    queries_in,
+    splices_in,
+    rope_in,
+    attended,
+    keys,
+    values,
+    arrived,
+    base_kv,
+    queries,
+    splices,
+    rope,
+    sem,
+):
+    loads = [
+        pltpu.make_async_copy(source, target, sem.at[i])
+        for i, (source, target) in enumerate(
+            (
+                (splices_in, splices),
+                (arrived_in, arrived),
+                (base_in, base_kv),
+                (rope_in, rope),
+                (queries_in, queries),
+            )
+        )
+    ]
+    for load in loads:
+        load.start()
+    n_configs, seq = keys.shape[0], keys.shape[1]
+    heads, n_cfg = queries.shape[0], arrived.shape[0]
     probe_row = lax.broadcasted_iota(jnp.int32, (heads * 8, seq), 0) & 7
     causal = lax.broadcasted_iota(jnp.int32, (heads * 8, seq), 1) <= seq - 8 + probe_row
-    settle(arrived.at[pl.ds(0, n_cfg - 1)], recv.at[6])
-
+    slots = n_cfg * 8
+    for load in loads:
+        load.wait()
+    probes = queries[...].reshape(heads * 8, HD).astype(bf16)
     spliced = arrived[...].astype(f32)
     taken_rows = jnp.concatenate(
         [spliced[:, :8, :].reshape(slots, HD), spliced[:, 8:, :].reshape(slots, HD)], axis=1
-    ).astype(bf16)
+    )
+    base_all = base_kv[...].astype(f32).reshape(seq, 2 * HD)
+    none = jnp.zeros((splices.shape[1] - slots - seq, 2 * HD), f32)
+    taken_rows = jnp.concatenate([taken_rows, base_all, none], axis=0).astype(bf16)
     for i in range(n_configs):
-        span = pl.ds(i * seq, seq)
-        taken = jnp.dot(placed[span, :], taken_rows, preferred_element_type=f32)
-        mixed = jnp.where(uncovered[span, :] > 0.5, base_all, taken)
+        splice = splices[pl.ds(i * seq, seq), :]
+        mixed = jnp.dot(splice, taken_rows, preferred_element_type=f32)
         key = rotate(mixed[:, :HD], rope[0], rope[1]).astype(bf16)
         value = mixed[:, HD:].astype(bf16)
         keys[i] = key
@@ -493,18 +612,20 @@
     tile = seq // group
     padded = -(-seq // HD) * HD
     vmem, anywhere = pl.BlockSpec(memory_space=pltpu.VMEM), pl.BlockSpec(memory_space=pl.ANY)
-    smem = pl.BlockSpec(memory_space=pltpu.SMEM)
     dma, hops = pltpu.SemaphoreType.DMA, n_tp - 1
-    return pl.pallas_call(
+    table = jnp.asarray(rope_tables(0, seq))
+    arrived, base_kv, queries, splices = pl.pallas_call(
         functools.partial(sweep_kernel, n_cfg, n_tp),
         out_shape=(
-            jax.ShapeDtypeStruct((n_configs, PROBE, heads * HD), bf16),
-            jax.ShapeDtypeStruct((n_configs, seq, HD), bf16),
-            jax.ShapeDtypeStruct((n_configs, seq, HD), bf16),
+            jax.ShapeDtypeStruct((n_cfg, TILE, HD), bf16),
+            jax.ShapeDtypeStruct((group, tile, 2 * HD), bf16),
+            jax.ShapeDtypeStruct((heads, 8, HD), f32),
+            jax.ShapeDtypeStruct((n_configs * seq, n_cfg * 8 + padded), bf16),
         ),
-        in_specs=[anywhere, smem] + [anywhere] * 8,
-        out_specs=(vmem, vmem, vmem),
+        in_specs=[anywhere] * 10,
+        out_specs=(anywhere,) * 4,
         scratch_shapes=[
+            pltpu.SMEM((1,), jnp.int32),
             pltpu.VMEM((n_tp, seq, width), bf16),
             pltpu.VMEM((n_tp * width, 2 * HD), bf16),
             pltpu.VMEM(w_query.shape, bf16),
@@ -514,30 +635,29 @@
             pltpu.VMEM((n_configs, cap, n_cfg), jnp.int32),
             pltpu.VMEM((n_configs, n_cfg), jnp.int32),
             pltpu.VMEM((2, seq, HD), f32),
+            pltpu.VMEM((n_configs * seq, n_cfg * 8 + padded), bf16),
             pltpu.VMEM((group, tile, width), bf16),
             pltpu.VMEM((group, tile, width), bf16),
             pltpu.VMEM((tile, width), bf16),
             pltpu.VMEM((n_cfg // group, tile, width), bf16),
             pltpu.VMEM((n_tp, tile, width), bf16),
-            pltpu.VMEM((tile, HD), bf16),
+            pltpu.VMEM((TILE, width), bf16),
+            pltpu.VMEM((n_cfg, TILE, HD), bf16),
+            pltpu.VMEM((TILE, HD), bf16),
             pltpu.VMEM((heads, TILE, HD), f32),
             pltpu.VMEM((n_cfg, TILE, HD), f32),
-            pltpu.VMEM((heads, 8, HD), f32),
-            pltpu.VMEM((group, tile, 2 * HD), bf16),
+            pltpu.VMEM((8, HD), f32),
+            pltpu.VMEM((tile, 2 * HD), bf16),
             pltpu.VMEM((n_cfg * TILE, 2 * padded), bf16),
-            pltpu.VMEM((n_configs * seq, n_cfg * 8), bf16),
-            pltpu.VMEM((n_configs * seq, 2 * HD), f32),
             pltpu.VMEM((2 * padded, HD), bf16),
-            pltpu.VMEM((n_cfg, TILE, HD), bf16),
             pltpu.VMEM((n_cfg, TILE, HD), bf16),
             pltpu.VMEM((seq, 2 * HD), f32),
             pltpu.VMEM((seq, HD), f32),
-            pltpu.VMEM((n_cfg, tile, 2 * HD), bf16),
-            dma((9,)),
+            dma((11,)),
             dma((2, hops)),
             dma((2, hops)),
-            dma((8,)),
-            dma((8,)),
+            dma((10,)),
+            dma((10,)),
         ],
         compiler_params=pltpu.CompilerParams(
             collective_id=0, has_side_effects=True, vmem_limit_bytes=60 << 20
@@ -550,10 +670,29 @@
         w_value,
         w_query,
         jnp.transpose(src_pos[:, 0, :], (1, 0)),
+        table,
         jnp.transpose(dst_pos, (0, 2, 1)),
         counts,
-        jnp.asarray(rope_tables(0, seq)),
     )
+    return pl.pallas_call(
+        attend_kernel,
+        out_shape=(
+            jax.ShapeDtypeStruct((n_configs, PROBE, heads * HD), bf16),
+            jax.ShapeDtypeStruct((n_configs, seq, HD), bf16),
+            jax.ShapeDtypeStruct((n_configs, seq, HD), bf16),
+        ),
+        in_specs=[anywhere] * 5,
+        out_specs=(vmem, vmem, vmem),
+        scratch_shapes=[
+            pltpu.VMEM(arrived.shape, bf16),
+            pltpu.VMEM(base_kv.shape, bf16),
+            pltpu.VMEM(queries.shape, f32),
+            pltpu.VMEM(splices.shape, bf16),
+            pltpu.VMEM(table.shape, f32),
+            dma((5,)),
+        ],
+        compiler_params=pltpu.CompilerParams(vmem_limit_bytes=60 << 20),
+    )(arrived, base_kv, queries, splices, table)
 
 
 def solution(mesh):

time: 76 us -> 66.9 us (0.88)
  Pallas kernels: 70 us -> 65.4 us
  local copies, waits for them, and re-layouts: 4.51 us -> 0 us
    pallas_call x1, Pallas kernels: 70 us -> 61.4 us  [body(): pl.pallas_call(functools.partial(sweep_kernel, n_cfg, n_tp), out_shape=(j...]
    unnamed x3 -> x0, local copies, waits for them, and re-layouts: 4.51 us -> none
    pallas_call x0 -> x1, Pallas kernels: none -> 4.04 us  [body(): pl.pallas_call(attend_kernel, out_shape=(jax.ShapeDtypeStruct((n_configs,...]
where the time goes in v3:
time: 66.9 us; the launch traced here: 66.7 us
  Pallas kernels  65.4 us (98%)
  between operations  1.29 us (2%)
    pallas_call x1, Pallas kernels, body(): pl.pallas_call(functools.partial(sweep_kernel, n_cfg, n_tp), out_shape=(j...  61.4 us
    pallas_call x1, Pallas kernels, body(): pl.pallas_call(attend_kernel, out_shape=(jax.ShapeDtypeStruct((n_configs,...  4.04 us

profile of v3, /device:TPU:1, one launch (start us, length us, event | category | flops | bytes accessed | tf_op | source)
XLA Modules:
  0.0 66.7 jit_solution(7958268445239743169)
XLA Ops:
  1.3 61.4 %shard_map.121 = (bf16[64,16,128]{2,1,0:T(8,128)(2,1)}, bf16[8,24,256]{2,1,0:T(8,128)(2,1)}, f32[8,8,128]{2,1,0:T(8,128)}, bf16[576,768]{1,0:T(8,128)(2,1)}) custom-call(bf16[192,1024]{1,0:T(8,128)(2,1)} %bitcast.6, s32[1]{0:T(128)S(6)} %copy.13.base_run, bf16[64,128]{1,0:T(8,128)(2,1)} %bitcast.7, bf16[8192,128]{1,0:T(8,128)(2,1)} %w_key.1, ...), custom_call_target="tpu_custom_call" | custom-call | tf_op jit(solution)/shard_map/pallas_call | solution.py:617
  62.7 4.0 %shard_map.122 = (bf16[3,4,1024]{2,1,0:T(4,128)(2,1)}, bf16[3,192,128]{2,1,0:T(8,128)(2,1)}, bf16[3,192,128]{2,1,0:T(8,128)(2,1)}) custom-call(bf16[64,16,128]{2,1,0:T(8,128)(2,1)} %get-tuple-element.7.arrived_in, bf16[8,24,256]{2,1,0:T(8,128)(2,1)} %get-tuple-element.8.base_in, f32[8,8,128]{2,1,0:T(8,128)} %get-tuple-element.9.queries_in, ...), custom_call_target="tpu_custom_call" | custom-call | tf_op jit(solution)/shard_map/pallas_call | solution.py:677

commit v4 on v3

--- a/solution.py
+++ b/solution.py
@@ -99,8 +99,14 @@
     group, tile = masked.shape[0], masked.shape[1]
     rings = n_cfg // group
     place, turn = lax.rem(cfg, group), cfg // group
-    holder = lax.rem(place, rings) * group + place
-    is_holder = cfg == holder
+    pieces = tile // 8
+
+    def holder(piece):
+        return lax.rem(place + 3 * piece, rings) * group + place
+
+    held = [cfg == holder(piece) for piece in range(pieces)]
+    is_holder = functools.reduce(jnp.logical_or, held)
+    my_piece = sum(piece * hit.astype(jnp.int32) for piece, hit in enumerate(held))
 
     def owner(head):
         return (head + rings // 2) % rings * group + head
@@ -143,15 +149,15 @@
 
     barrier = pltpu.get_barrier_semaphore()
 
-    @pl.loop(0, n_cfg - 1)
-    def _(i):
-        pl.semaphore_signal(barrier, inc=1, device_id={"cfg": peer(i)}, device_id_type=MESH)
-
     @pl.loop(1, n_tp)
     def _(i):
         pl.semaphore_signal(
             barrier, inc=1, device_id={"tp": lax.rem(tp + i, n_tp)}, device_id_type=MESH
         )
+
+    @pl.loop(0, n_cfg - 1)
+    def _(i):
+        pl.semaphore_signal(barrier, inc=1, device_id={"cfg": peer(i)}, device_id_type=MESH)
 
     loads[0].wait()
     loads[1].wait()
@@ -176,6 +182,10 @@
             device_id={"cfg": target},
             device_id_type=MESH,
         )
+
+    def both(condition, if_true, if_false):
+        pl.when(condition)(if_true)
+        pl.when(jnp.logical_not(condition))(if_false)
 
     def settle(ref, sem):
         pltpu.make_async_copy(ref, ref, sem).wait()
@@ -316,15 +326,16 @@
         total = row_sums[0].astype(f32)
         for q in range(1, group):
             total += row_sums[q].astype(f32)
-        middle[...] = total.astype(bf16)
-
-        @pl.when(jnp.logical_not(is_holder))
-        def _():
-            to_cfg(middle, landed.at[turn], 7, holder).start()
-
-        @pl.when(is_holder)
-        def _():
-            landed[turn] = middle[...]
+        for piece in range(pieces):
+            middle[piece] = total[piece * 8 : (piece + 1) * 8, :].astype(bf16)
+
+            @pl.when(jnp.logical_not(held[piece]))
+            def _():
+                to_cfg(middle.at[piece], landed.at[turn], 7, holder(piece)).start()
+
+            @pl.when(held[piece])
+            def _():
+                landed[turn] = middle[piece]
 
     def place_slots():
         slots = n_cfg * 8
@@ -384,20 +395,23 @@
                 return total, squares + lane_groups(wide * wide)
 
             total, squares = lax.fori_loop(
-                0, n_tp, add, (jnp.zeros((tile, 2 * HD), f32), jnp.zeros((tile, HD), f32))
+                0, n_tp, add, (jnp.zeros((8, 2 * HD), f32), jnp.zeros((8, HD), f32))
             )
             scale = lax.rsqrt(jnp.sum(squares, axis=1, keepdims=True) / model + EPSILON)
-            my_base_kv[...] = (total * scale).astype(bf16)
+            my_base_kv[my_piece] = (total * scale).astype(bf16)
 
             @pl.loop(0, rings - 1)
             def _(i):
                 other = lax.rem(turn + outward(i, rings), rings)
-                to_cfg(my_base_kv, my_base_kv, 3, other * group + place).start()
+                mine = my_base_kv.at[my_piece]
+                to_cfg(mine, mine, 3, other * group + place).start()
 
     def base_spreads():
-        @pl.when(jnp.logical_not(is_holder))
-        def _():
-            settle(my_base_kv, recv.at[3])
+        both(
+            is_holder,
+            lambda: settle(my_base_kv.at[pl.ds(0, pieces - 1)], recv.at[3]),
+            lambda: settle(my_base_kv, recv.at[3]),
+        )
 
         @pl.loop(1, group)
         def _(i):
@@ -472,34 +486,41 @@
     scaled = (acc[...] * scale).astype(bf16)
     kv[pl.ds(0, seq), :] = scaled[:, :HD]
     kv[pl.ds(padded, seq), :] = scaled[:, HD:]
-    picked = jnp.dot(chosen[...], kv[...], preferred_element_type=f32).astype(bf16)
-    outgoing[...] = picked.reshape(n_cfg, TILE, HD)
-
-    @pl.loop(0, n_cfg - 1)
-    def _(i):
-        target = peer(i)
-        to_cfg(outgoing.at[target], arrived.at[cfg], 6, target).start()
+
+    @pl.loop(0, rings)
+    def _(step):
+        first = lax.rem(turn + outward(step, rings), rings) * group
+        span = pl.ds(pl.multiple_of(first * TILE, TILE * group), TILE * group)
+        picked = jnp.dot(chosen[span, :], kv[...], preferred_element_type=f32).astype(bf16)
+        outgoing[pl.ds(first, group)] = picked.reshape(group, TILE, HD)
+
+        @pl.loop(0, group)
+        def _(across):
+            x = lax.rem(lax.div(place, 2) + outward(lax.div(across, 2), group // 2), group // 2)
+            target = first + x * 2 + lax.rem(place + 1 - lax.rem(across, 2), 2)
+
+            @pl.when(target != cfg)
+            def _():
+                to_cfg(outgoing.at[target], arrived.at[cfg], 6, target).start()
 
     own = pltpu.make_async_copy(outgoing.at[cfg], arrived.at[cfg], load_sem.at[2])
     own.start()
-
-    def both(condition, if_true, if_false):
-        pl.when(condition)(if_true)
-        pl.when(jnp.logical_not(condition))(if_false)
 
     for unit in range(units):
         for direction in (0, 1):
             ring(direction, unit).wait_send()
     settle(masked.at[pl.ds(0, group - 1)], send.at[0])
 
-    @pl.when(jnp.logical_not(is_holder))
-    def _():
-        settle(middle, send.at[7])
+    both(
+        is_holder,
+        lambda: settle(middle.at[pl.ds(0, pieces - 1)], send.at[7]),
+        lambda: settle(middle, send.at[7]),
+    )
 
     @pl.when(is_holder)
     def _():
         settle(base_rows.at[pl.ds(0, n_tp - 1)], send.at[1])
-        settle(base_kv.at[pl.ds(0, rings - 1)], send.at[3])
+        settle(base_kv.at[pl.ds(0, rings - 1), 0], send.at[3])
 
     both(
         makes_block,
@@ -546,6 +567,9 @@
     queries_in,
     splices_in,
     rope_in,
+    attended_out,
+    keys_out,
+    values_out,
     attended,
     keys,
     values,
@@ -585,13 +609,21 @@
     base_all = base_kv[...].astype(f32).reshape(seq, 2 * HD)
     none = jnp.zeros((splices.shape[1] - slots - seq, 2 * HD), f32)
     taken_rows = jnp.concatenate([taken_rows, base_all, none], axis=0).astype(bf16)
+    mixed = jnp.dot(splices[...], taken_rows, preferred_element_type=f32)
     for i in range(n_configs):
-        splice = splices[pl.ds(i * seq, seq), :]
-        mixed = jnp.dot(splice, taken_rows, preferred_element_type=f32)
-        key = rotate(mixed[:, :HD], rope[0], rope[1]).astype(bf16)
-        value = mixed[:, HD:].astype(bf16)
-        keys[i] = key
-        values[i] = value
+        row = mixed[i * seq : (i + 1) * seq, :]
+        keys[i] = rotate(row[:, :HD], rope[0], rope[1]).astype(bf16)
+        values[i] = row[:, HD:].astype(bf16)
+    stores = [
+        pltpu.make_async_copy(source, target, sem.at[i])
+        for i, (source, target) in enumerate(
+            ((keys, keys_out), (values, values_out), (attended, attended_out))
+        )
+    ]
+    stores[0].start()
+    stores[1].start()
+    for i in range(n_configs):
+        key, value = keys[i], values[i]
         scores = lax.dot_general(
             probes, key, (((1,), (1,)), ((), ())), preferred_element_type=f32
         ) * HD ** (-0.5)
@@ -602,6 +634,9 @@
         out = jnp.dot(probs, value, preferred_element_type=f32)
         for h in range(heads):
             attended[i, :, h * HD : (h + 1) * HD] = out[h * 8 + 8 - PROBE : h * 8 + 8, :].astype(bf16)
+    stores[2].start()
+    for store in stores:
+        store.wait()
 
 
 def body(n_cfg, n_tp, pool, base_run, gain, w_key, w_value, w_query, src_pos, dst_pos, counts):
@@ -611,14 +646,14 @@
     group = 1 << (n_cfg.bit_length() // 2)
     tile = seq // group
     padded = -(-seq // HD) * HD
-    vmem, anywhere = pl.BlockSpec(memory_space=pltpu.VMEM), pl.BlockSpec(memory_space=pl.ANY)
+    anywhere = pl.BlockSpec(memory_space=pl.ANY)
     dma, hops = pltpu.SemaphoreType.DMA, n_tp - 1
     table = jnp.asarray(rope_tables(0, seq))
     arrived, base_kv, queries, splices = pl.pallas_call(
         functools.partial(sweep_kernel, n_cfg, n_tp),
         out_shape=(
             jax.ShapeDtypeStruct((n_cfg, TILE, HD), bf16),
-            jax.ShapeDtypeStruct((group, tile, 2 * HD), bf16),
+            jax.ShapeDtypeStruct((group, tile // 8, 8, 2 * HD), bf16),
             jax.ShapeDtypeStruct((heads, 8, HD), f32),
             jax.ShapeDtypeStruct((n_configs * seq, n_cfg * 8 + padded), bf16),
         ),
@@ -638,16 +673,16 @@
             pltpu.VMEM((n_configs * seq, n_cfg * 8 + padded), bf16),
             pltpu.VMEM((group, tile, width), bf16),
             pltpu.VMEM((group, tile, width), bf16),
-            pltpu.VMEM((tile, width), bf16),
-            pltpu.VMEM((n_cfg // group, tile, width), bf16),
-            pltpu.VMEM((n_tp, tile, width), bf16),
+            pltpu.VMEM((tile // 8, 8, width), bf16),
+            pltpu.VMEM((n_cfg // group, 8, width), bf16),
+            pltpu.VMEM((n_tp, 8, width), bf16),
             pltpu.VMEM((TILE, width), bf16),
             pltpu.VMEM((n_cfg, TILE, HD), bf16),
             pltpu.VMEM((TILE, HD), bf16),
             pltpu.VMEM((heads, TILE, HD), f32),
             pltpu.VMEM((n_cfg, TILE, HD), f32),
             pltpu.VMEM((8, HD), f32),
-            pltpu.VMEM((tile, 2 * HD), bf16),
+            pltpu.VMEM((tile // 8, 8, 2 * HD), bf16),
             pltpu.VMEM((n_cfg * TILE, 2 * padded), bf16),
             pltpu.VMEM((2 * padded, HD), bf16),
             pltpu.VMEM((n_cfg, TILE, HD), bf16),
@@ -682,8 +717,11 @@
             jax.ShapeDtypeStruct((n_configs, seq, HD), bf16),
         ),
         in_specs=[anywhere] * 5,
-        out_specs=(vmem, vmem, vmem),
+        out_specs=(anywhere,) * 3,
         scratch_shapes=[
+            pltpu.VMEM((n_configs, PROBE, heads * HD), bf16),
+            pltpu.VMEM((n_configs, seq, HD), bf16),
+            pltpu.VMEM((n_configs, seq, HD), bf16),
             pltpu.VMEM(arrived.shape, bf16),
             pltpu.VMEM(base_kv.shape, bf16),
             pltpu.VMEM(queries.shape, f32),

time: 66.9 us -> 65.1 us (0.973)
  Pallas kernels: 65.4 us -> 63.7 us
    pallas_call x1, Pallas kernels: 61.4 us -> 60 us  [body(): pl.pallas_call(functools.partial(sweep_kernel, n_cfg, n_tp), out_shape=(j...]
where the time goes in v4:
time: 65.1 us; the launch traced here: 65 us
  Pallas kernels  63.7 us (98%)
  between operations  1.29 us (2%)
    pallas_call x1, Pallas kernels, body(): pl.pallas_call(functools.partial(sweep_kernel, n_cfg, n_tp), out_shape=(j...  60 us
    pallas_call x1, Pallas kernels, body(): pl.pallas_call(attend_kernel, out_shape=(jax.ShapeDtypeStruct((n_configs,...  3.67 us

profile of v4, /device:TPU:1, one launch (start us, length us, event | category | flops | bytes accessed | tf_op | source)
XLA Modules:
  0.0 65.0 jit_solution(16046721296335286304)
XLA Ops:
  1.3 60.0 %shard_map.121 = (bf16[64,16,128]{2,1,0:T(8,128)(2,1)}, bf16[8,3,8,256]{3,2,1,0:T(8,128)(2,1)}, f32[8,8,128]{2,1,0:T(8,128)}, bf16[576,768]{1,0:T(8,128)(2,1)}) custom-call(bf16[192,1024]{1,0:T(8,128)(2,1)} %bitcast.6, s32[1]{0:T(128)S(6)} %copy.13.base_run, bf16[64,128]{1,0:T(8,128)(2,1)} %bitcast.7, bf16[8192,128]{1,0:T(8,128)(2,1)} %w_key.1, ...), custom_call_target="tpu_custom_call" | custom-call | tf_op jit(solution)/shard_map/pallas_call | solution.py:652
  61.3 3.7 %shard_map.122 = (bf16[3,4,1024]{2,1,0:T(4,128)(2,1)}, bf16[3,192,128]{2,1,0:T(8,128)(2,1)}, bf16[3,192,128]{2,1,0:T(8,128)(2,1)}) custom-call(bf16[64,16,128]{2,1,0:T(8,128)(2,1)} %get-tuple-element.7.arrived_in, bf16[8,3,8,256]{3,2,1,0:T(8,128)(2,1)} %get-tuple-element.8.base_in, f32[8,8,128]{2,1,0:T(8,128)} %get-tuple-element.9.queries_in, ...), custom_call_target="tpu_custom_call" | custom-call | tf_op jit(solution)/shard_map/pallas_call | solution.py:712

commit v5 on v4

--- a/solution.py
+++ b/solution.py
@@ -459,19 +459,35 @@
                 total[:8] * scale, rope[0, pl.ds(seq - 8, 8), :], rope[1, pl.ds(seq - 8, 8), :]
             )
 
+
+            @pl.loop(0, rings - 1)
+            def _(i):
+                other = lax.rem(turn + outward(i, rings), rings)
+                to_cfg(my_queries, my_queries, 5, other * group + place).start()
+
+    passes_on = place < heads
+
+    def query_spreads():
+        @pl.when(jnp.logical_and(passes_on, jnp.logical_not(is_owner)))
+        def _():
+            settle(my_queries, recv.at[5])
+
+        @pl.when(passes_on)
+        def _():
             pltpu.make_async_copy(my_queries, queries.at[my_head], load_sem.at[1]).start()
 
-            @pl.loop(0, n_cfg - 1)
+            @pl.loop(1, group)
             def _(i):
-                to_cfg(my_queries, queries.at[my_head], 5, peer(i)).start()
+                other = lax.rem(place + i, group)
+                to_cfg(my_queries, queries.at[my_head], 10, turn * group + other).start()
 
     beside = [
         (probes_meet, base_meets),
         (base_arrives, query_parts),
-        (place_slots,),
         (base_projects,),
         (query_sums,),
         (base_spreads,),
+        (query_spreads, place_slots),
     ]
     for unit in range(max(units, len(beside))):
         if unit < units:
@@ -540,14 +556,18 @@
     settle(base_kv.at[pl.ds(0, group - 1)], send.at[9])
     settle(base_kv.at[pl.ds(0, group - 1)], recv.at[9])
     both(
-        is_owner,
-        lambda: settle(queries.at[pl.ds(0, heads - 1)], recv.at[5]),
-        lambda: settle(queries, recv.at[5]),
+        passes_on,
+        lambda: settle(queries.at[pl.ds(0, heads - 1)], recv.at[10]),
+        lambda: settle(queries, recv.at[10]),
     )
 
     @pl.when(is_owner)
     def _():
-        settle(arrived.at[pl.ds(0, n_cfg - 1)], send.at[5])
+        settle(arrived.at[pl.ds(0, rings - 1)], send.at[5])
+
+    @pl.when(passes_on)
+    def _():
+        settle(arrived.at[pl.ds(0, group - 1)], send.at[10])
 
     settle(outgoing.at[pl.ds(0, n_cfg - 1)], send.at[6])
     settle(arrived.at[pl.ds(0, n_cfg - 1)], recv.at[6])
@@ -556,7 +576,7 @@
 
     pltpu.make_async_copy(my_base_kv, base_kv.at[place], load_sem.at[0]).wait()
 
-    @pl.when(is_owner)
+    @pl.when(passes_on)
     def _():
         pltpu.make_async_copy(my_queries, queries.at[my_head], load_sem.at[1]).wait()
 
@@ -691,8 +711,8 @@
             dma((11,)),
             dma((2, hops)),
             dma((2, hops)),
-            dma((10,)),
-            dma((10,)),
+            dma((11,)),
+            dma((11,)),
         ],
         compiler_params=pltpu.CompilerParams(
             collective_id=0, has_side_effects=True, vmem_limit_bytes=60 << 20

time: 65.1 us -> 65.1 us (level)
  no operation moved by 1% of the time
where the time goes in v5:
time: 65.1 us; the launch traced here: 65 us
  Pallas kernels  63.7 us (98%)
  between operations  1.29 us (2%)
    pallas_call x1, Pallas kernels, body(): pl.pallas_call(functools.partial(sweep_kernel, n_cfg, n_tp), out_shape=(j...  60 us
    pallas_call x1, Pallas kernels, body(): pl.pallas_call(attend_kernel, out_shape=(jax.ShapeDtypeStruct((n_configs,...  3.67 us

profile of v5, /device:TPU:1, one launch (start us, length us, event | category | flops | bytes accessed | tf_op | source)
XLA Modules:
  0.0 65.0 jit_solution(4814367633159840656)
XLA Ops:
  1.3 60.0 %shard_map.121 = (bf16[64,16,128]{2,1,0:T(8,128)(2,1)}, bf16[8,3,8,256]{3,2,1,0:T(8,128)(2,1)}, f32[8,8,128]{2,1,0:T(8,128)}, bf16[576,768]{1,0:T(8,128)(2,1)}) custom-call(bf16[192,1024]{1,0:T(8,128)(2,1)} %bitcast.6, s32[1]{0:T(128)S(6)} %copy.13.base_run, bf16[64,128]{1,0:T(8,128)(2,1)} %bitcast.7, bf16[8192,128]{1,0:T(8,128)(2,1)} %w_key.1, ...), custom_call_target="tpu_custom_call" | custom-call | tf_op jit(solution)/shard_map/pallas_call | solution.py:672
  61.3 3.7 %shard_map.122 = (bf16[3,4,1024]{2,1,0:T(4,128)(2,1)}, bf16[3,192,128]{2,1,0:T(8,128)(2,1)}, bf16[3,192,128]{2,1,0:T(8,128)(2,1)}) custom-call(bf16[64,16,128]{2,1,0:T(8,128)(2,1)} %get-tuple-element.7.arrived_in, bf16[8,3,8,256]{3,2,1,0:T(8,128)(2,1)} %get-tuple-element.8.base_in, f32[8,8,128]{2,1,0:T(8,128)} %get-tuple-element.9.queries_in, ...), custom_call_target="tpu_custom_call" | custom-call | tf_op jit(solution)/shard_map/pallas_call | solution.py:732
